TPU v7x, 256 devices: a whole 4x4x8 slice. The times are simulated.
256 devices in a mesh: sta: 32 (over z, y_lo, core), freq: 8 (over x, y_hi).
Axes of the slice: x: 4, y: 4 (y_hi: 2, y_lo: 2; y = y_hi * 2 + y_lo), z: 8, core: 2. Of those that a mesh axis runs over, the one named last changes fastest.
Arguments:
- spectra: bfloat16 [2, 768, 4096], P(None, 'sta', 'freq'), may hold values from -6 to 6
- pair_mask: int32 [32, 32], replicated, may hold values from 0 to 1, as said below
Outputs:
- correlograms: bfloat16 [32, 17, 24, 24, 512], P('sta', None, 'freq')
Inputs may be any that keep to these rules, and one draw needn't show every extreme that they name: pair_mask is symmetric and its diagonal is 1.
All inputs are finite; a program needn't handle non-finite values.
Results may differ from a plain program's by a relative error of at most 0.0055.
Values may be sent and summed in bfloat16 or wider, within the bound.
A program may use at most 64 MiB of HBM per device.

v0:
```python
import math

import jax
import jax.numpy as jnp
from jax import lax
from jax.sharding import PartitionSpec as P

FREQS = 4096
LAGS = 512


def shifted(value, axis, steps):
    count = lax.axis_size(axis)
    pairs = [(source, (source + steps) % count) for source in range(count)]
    return lax.ppermute(value, axis, pairs)


def lag_table(count):
    bins = jnp.arange(count, dtype=jnp.int32)
    shifts = jnp.arange(LAGS, dtype=jnp.int32) - LAGS // 2
    phase = bins[:, None] * shifts[None, :] % (2 * FREQS)
    angle = math.pi * phase.astype(jnp.float32) / FREQS
    factor = 1.0 / math.sqrt(FREQS)
    return jnp.concatenate([jnp.cos(angle) * factor, -jnp.sin(angle) * factor], axis=0).astype(
        jnp.bfloat16
    )


def cross_spectra(mine, other):
    real_a = mine[0].astype(jnp.float32)[:, None, :]
    imag_a = mine[1].astype(jnp.float32)[:, None, :]
    real_b = other[0].astype(jnp.float32)[None, :, :]
    imag_b = other[1].astype(jnp.float32)[None, :, :]
    real_part = real_a * real_b + imag_a * imag_b
    imag_part = imag_a * real_b - real_a * imag_b
    return jnp.concatenate([real_part, imag_part], axis=2).astype(jnp.bfloat16)


def project(mine, other, table, flag):
    count = mine.shape[1]
    members = other.shape[1]
    width = mine.shape[2]

    def compute(operands):
        product = cross_spectra(operands[0], operands[1]).reshape(count * members, 2 * width)
        return jnp.dot(product, table, preferred_element_type=jnp.float32).reshape(
            count, members, LAGS
        )

    def nothing(operands):
        return jnp.zeros((count, members, LAGS), jnp.float32)

    return lax.cond(flag > 0, compute, nothing, (mine, other))


def local(spectra, pair_mask):
    groups = lax.axis_size("freq")
    band_index = lax.axis_index("freq")
    cycle = lax.axis_size("sta")
    block = lax.axis_index("sta")
    members = spectra.shape[1]
    own_rows = members // groups
    first_row = band_index * own_rows
    distinct = (first_row + jnp.arange(own_rows, dtype=jnp.int32))[:, None] != jnp.arange(
        members, dtype=jnp.int32
    )[None, :]
    moving = lax.all_gather(spectra, "freq", axis=2, tiled=True)
    table = lag_table(FREQS)
    mine = lax.dynamic_slice_in_dim(moving, first_row, own_rows, 1)

    def correlate(partner, offset):
        flag = pair_mask[block, (block + offset) % cycle]
        return project(mine, partner, table, flag)

    def finish(value, offset):
        keep = jnp.logical_or(offset != 0, distinct)
        return jnp.where(keep[:, :, None], value, 0.0).astype(jnp.bfloat16)

    first = finish(correlate(moving, 0), 0)[None]

    def advance(carry, offset):
        partner = shifted(carry, "sta", -1)
        return (partner, finish(correlate(partner, offset), offset))

    rest = lax.scan(advance, moving, jnp.arange(1, cycle // 2 + 1, dtype=jnp.int32))[1]
    stacked = jnp.concatenate([first, rest], axis=0)
    return stacked[None]


def solution(mesh):
    return jax.shard_map(
        local,
        mesh=mesh,
        in_specs=(P(None, "sta", "freq"), P()),
        out_specs=P("sta", None, "freq", None, None),
        check_vma=False,
    )
```

profile of v0, /device:TPU:121, one launch (start us, length us, event | category | flops | bytes accessed | tf_op | source)
XLA Modules:
  0.0 288.1 jit_solution(7775883402093495422)
XLA Ops:
  1.9 29.0 %all_gather.3 = bf16[2,24,4096]{2,1,0:T(8,128)(2,1)S(1)} all-gather(bf16[2,24,512]{2,1,0:T(8,128)(2,1)} %param.8), channel_id=1, replica_groups=mesh['sta'=32,'freq'=8] {'freq'}, dimensions={2}, use_global_device_ids=true | all-gather | bytes 442368 | tf_op jit(solution)/shard_map/all_gather | solution.py:67
  31.0 35.3 %multiply_convert_fusion.1 = (bf16[4096,512]{1,0:T(8,128)(2,1)}, bf16[4096,512]{1,0:T(8,128)(2,1)}) fusion(s32[512]{0:T(512)S(1)} %iota_add_fusion), kind=kLoop, calls=%fused_computation.38 | loop fusion | flops 39845888 | bytes 8390656 | tf_op jit(solution)/shard_map/convert.14
  66.3 7.2 %pad_maximum_fusion = bf16[8192,512]{1,0:T(8,128)(2,1)} fusion(bf16[4096,512]{1,0:T(8,128)(2,1)} %get-tuple-element.211, bf16[4096,512]{1,0:T(8,128)(2,1)} %get-tuple-element.210), kind=kLoop, calls=%fused_computation.36 | loop fusion | flops 16777216 | bytes 16777216 | tf_op jit(solution)/shard_map/concatenate | solution.py:24
  73.5 5.3 %conditional.2 = (bf16[3,24,512]{2,1,0:T(8,128)(2,1)S(1)}) conditional(s32[]{:T(128)} %bitcast.10, () %tuple.29, (bf16[2,3,4096]{2,1,0:T(4,128)(2,1)S(1)}, bf16[2,24,4096]{2,1,0:T(8,128)(2,1)S(1)}, bf16[8192,512]{1,0:T(8,128)(2,1)}) %tuple.30), branch_computations={%region_0.1_spmd, %region_1.2_spmd} | conditional | flops 608919552 | bytes 13033480 | solution.py:53
  73.9 5.0 %fusion.2 = bf16[3,24,512]{2,1,0:T(8,128)(2,1)S(1)} fusion(bf16[8192,512]{1,0:T(8,128)(2,1)} %get-tuple-element.138, bf16[3,24,4096]{2,1,0:T(8,128)(2,1)S(1)} %get-tuple-element.199, bf16[3,24,4096]{2,1,0:T(8,128)(2,1)S(1)} %get-tuple-element.198), kind=kOutput, calls=%fused_computation.1 | convolution fusion | flops 606339072 | bytes 9641984 | tf_op jit(solution)/shard_map/cond/branch_1_fun/dot_general | solution.py:46
  79.0 207.9 %while.15 = (s32[]{:T(128)}, bf16[2,24,4096]{2,1,0:T(8,128)(2,1)S(1)}, bf16[16,3,24,512]{3,2,1,0:T(8,128)(2,1)S(1)}, s32[16]{0:T(128)S(1)}, s32[]{:T(128)}, /*in...) while((s32[]{:T(128)}, ...), condition=%wide.region_5.6_spmd.clone, body=%wide.region_2.5_spmd.clone.sunk | while | flops 608956544 | bytes 15541248 | solution.py:85
  79.1 6.9 %collective-permute-start = (bf16[2,24,4096]{2,1,0:T(8,128)(2,1)S(1)}, bf16[2,24,4096]{2,1,0:T(8,128)(2,1)S(1)}, u32[]{:S(2)}, u32[]{:S(2)}) collective-permute-start(bf16[2,24,4096]{2,1,0:T(8,128)(2,1)S(1)} %get-tuple-element.289), channel_id=1, source_target_pairs={{0,248},{8,0},{16,8},{24,16},{32,24},{40,32},{48,40},{56,48},{64,5... | collective-permute-start | bytes 1179656 | tf_op jit(solution)/shard_map/while/body/eval_jaxpr/ppermute | solution.py:15
  89.9 4.5 %collective-permute-done = bf16[2,24,4096]{2,1,0:T(8,128)(2,1)S(1)} collective-permute-done((bf16[2,24,4096]{2,1,0:T(8,128)(2,1)S(1)}, bf16[2,24,4096]{2,1,0:T(8,128)(2,1)S(1)}, u32[]{:S(2)}, u32[]{:S(2)}) %collective-permute-start) | collective-permute-done | bytes 393248 | tf_op jit(solution)/shard_map/while/body/eval_jaxpr/ppermute | solution.py:15
  94.3 5.3 %conditional.5 = (bf16[3,24,512]{2,1,0:T(8,128)(2,1)S(1)}) conditional(s32[]{:T(128)} %bitcast.46, () %tuple.54, (bf16[2,3,4096]{2,1,0:T(4,128)(2,1)S(1)}, bf16[2,24,4096]{2,1,0:T(8,128)(2,1)S(1)}, bf16[8192,512]{1,0:T(8,128)(2,1)}) %tuple.55), branch_computations={%region_3.3_spmd, %region_4.4_spmd} | conditional | flops 608919552 | bytes 13033480 | solution.py:53
  94.7 5.0 %fusion.8 = bf16[3,24,512]{2,1,0:T(8,128)(2,1)S(1)} fusion(bf16[8192,512]{1,0:T(8,128)(2,1)} %get-tuple-element.141, bf16[3,24,4096]{2,1,0:T(8,128)(2,1)S(1)} %get-tuple-element.205, bf16[3,24,4096]{2,1,0:T(8,128)(2,1)S(1)} %get-tuple-element.204), kind=kOutput, calls=%fused_computation.13 | convolution fusion | flops 606339072 | bytes 9641984 | tf_op jit(solution)/shard_map/while/body/eval_jaxpr/cond/branch_1_fun/dot_general | solution.py:46
  101.8 1.3 dynamic_slice.27
  103.8 5.4 %collective-permute-done = bf16[2,24,4096]{2,1,0:T(8,128)(2,1)S(1)} collective-permute-done((bf16[2,24,4096]{2,1,0:T(8,128)(2,1)S(1)}, bf16[2,24,4096]{2,1,0:T(8,128)(2,1)S(1)}, u32[]{:S(2)}, u32[]{:S(2)}) %collective-permute-start) | collective-permute-done | bytes 393248 | tf_op jit(solution)/shard_map/while/body/eval_jaxpr/ppermute | solution.py:15
  111.4 1.3 dynamic_slice.27
  113.4 6.7 %collective-permute-done = bf16[2,24,4096]{2,1,0:T(8,128)(2,1)S(1)} collective-permute-done((bf16[2,24,4096]{2,1,0:T(8,128)(2,1)S(1)}, bf16[2,24,4096]{2,1,0:T(8,128)(2,1)S(1)}, u32[]{:S(2)}, u32[]{:S(2)}) %collective-permute-start) | collective-permute-done | bytes 393248 | tf_op jit(solution)/shard_map/while/body/eval_jaxpr/ppermute | solution.py:15
  124.2 6.7 %collective-permute-done = bf16[2,24,4096]{2,1,0:T(8,128)(2,1)S(1)} collective-permute-done((bf16[2,24,4096]{2,1,0:T(8,128)(2,1)S(1)}, bf16[2,24,4096]{2,1,0:T(8,128)(2,1)S(1)}, u32[]{:S(2)}, u32[]{:S(2)}) %collective-permute-start) | collective-permute-done | bytes 393248 | tf_op jit(solution)/shard_map/while/body/eval_jaxpr/ppermute | solution.py:15
  131.0 5.3 %conditional.5 = (bf16[3,24,512]{2,1,0:T(8,128)(2,1)S(1)}) conditional(s32[]{:T(128)} %bitcast.46, () %tuple.54, (bf16[2,3,4096]{2,1,0:T(4,128)(2,1)S(1)}, bf16[2,24,4096]{2,1,0:T(8,128)(2,1)S(1)}, bf16[8192,512]{1,0:T(8,128)(2,1)}) %tuple.55), branch_computations={%region_3.3_spmd, %region_4.4_spmd} | conditional | flops 608919552 | bytes 13033480 | solution.py:53
  131.3 5.0 %fusion.8 = bf16[3,24,512]{2,1,0:T(8,128)(2,1)S(1)} fusion(bf16[8192,512]{1,0:T(8,128)(2,1)} %get-tuple-element.141, bf16[3,24,4096]{2,1,0:T(8,128)(2,1)S(1)} %get-tuple-element.205, bf16[3,24,4096]{2,1,0:T(8,128)(2,1)S(1)} %get-tuple-element.204), kind=kOutput, calls=%fused_computation.13 | convolution fusion | flops 606339072 | bytes 9641984 | tf_op jit(solution)/shard_map/while/body/eval_jaxpr/cond/branch_1_fun/dot_general | solution.py:46
  138.4 1.3 dynamic_slice.27
  140.4 5.4 %collective-permute-done = bf16[2,24,4096]{2,1,0:T(8,128)(2,1)S(1)} collective-permute-done((bf16[2,24,4096]{2,1,0:T(8,128)(2,1)S(1)}, bf16[2,24,4096]{2,1,0:T(8,128)(2,1)S(1)}, u32[]{:S(2)}, u32[]{:S(2)}) %collective-permute-start) | collective-permute-done | bytes 393248 | tf_op jit(solution)/shard_map/while/body/eval_jaxpr/ppermute | solution.py:15
  145.8 5.3 %conditional.5 = (bf16[3,24,512]{2,1,0:T(8,128)(2,1)S(1)}) conditional(s32[]{:T(128)} %bitcast.46, () %tuple.54, (bf16[2,3,4096]{2,1,0:T(4,128)(2,1)S(1)}, bf16[2,24,4096]{2,1,0:T(8,128)(2,1)S(1)}, bf16[8192,512]{1,0:T(8,128)(2,1)}) %tuple.55), branch_computations={%region_3.3_spmd, %region_4.4_spmd} | conditional | flops 608919552 | bytes 13033480 | solution.py:53
  146.2 5.0 %fusion.8 = bf16[3,24,512]{2,1,0:T(8,128)(2,1)S(1)} fusion(bf16[8192,512]{1,0:T(8,128)(2,1)} %get-tuple-element.141, bf16[3,24,4096]{2,1,0:T(8,128)(2,1)S(1)} %get-tuple-element.205, bf16[3,24,4096]{2,1,0:T(8,128)(2,1)S(1)} %get-tuple-element.204), kind=kOutput, calls=%fused_computation.13 | convolution fusion | flops 606339072 | bytes 9641984 | tf_op jit(solution)/shard_map/while/body/eval_jaxpr/cond/branch_1_fun/dot_general | solution.py:46
  153.3 1.3 dynamic_slice.27
  155.3 5.4 %collective-permute-done = bf16[2,24,4096]{2,1,0:T(8,128)(2,1)S(1)} collective-permute-done((bf16[2,24,4096]{2,1,0:T(8,128)(2,1)S(1)}, bf16[2,24,4096]{2,1,0:T(8,128)(2,1)S(1)}, u32[]{:S(2)}, u32[]{:S(2)}) %collective-permute-start) | collective-permute-done | bytes 393248 | tf_op jit(solution)/shard_map/while/body/eval_jaxpr/ppermute | solution.py:15
  162.9 1.3 dynamic_slice.27
  164.9 5.4 %collective-permute-done = bf16[2,24,4096]{2,1,0:T(8,128)(2,1)S(1)} collective-permute-done((bf16[2,24,4096]{2,1,0:T(8,128)(2,1)S(1)}, bf16[2,24,4096]{2,1,0:T(8,128)(2,1)S(1)}, u32[]{:S(2)}, u32[]{:S(2)}) %collective-permute-start) | collective-permute-done | bytes 393248 | tf_op jit(solution)/shard_map/while/body/eval_jaxpr/ppermute | solution.py:15
  172.4 1.3 dynamic_slice.27
  174.4 6.7 %collective-permute-done = bf16[2,24,4096]{2,1,0:T(8,128)(2,1)S(1)} collective-permute-done((bf16[2,24,4096]{2,1,0:T(8,128)(2,1)S(1)}, bf16[2,24,4096]{2,1,0:T(8,128)(2,1)S(1)}, u32[]{:S(2)}, u32[]{:S(2)}) %collective-permute-start) | collective-permute-done | bytes 393248 | tf_op jit(solution)/shard_map/while/body/eval_jaxpr/ppermute | solution.py:15
  183.3 1.3 dynamic_slice.27
  185.3 5.4 %collective-permute-done = bf16[2,24,4096]{2,1,0:T(8,128)(2,1)S(1)} collective-permute-done((bf16[2,24,4096]{2,1,0:T(8,128)(2,1)S(1)}, bf16[2,24,4096]{2,1,0:T(8,128)(2,1)S(1)}, u32[]{:S(2)}, u32[]{:S(2)}) %collective-permute-start) | collective-permute-done | bytes 393248 | tf_op jit(solution)/shard_map/while/body/eval_jaxpr/ppermute | solution.py:15
  192.8 1.3 dynamic_slice.27
  194.8 6.7 %collective-permute-done = bf16[2,24,4096]{2,1,0:T(8,128)(2,1)S(1)} collective-permute-done((bf16[2,24,4096]{2,1,0:T(8,128)(2,1)S(1)}, bf16[2,24,4096]{2,1,0:T(8,128)(2,1)S(1)}, u32[]{:S(2)}, u32[]{:S(2)}) %collective-permute-start) | collective-permute-done | bytes 393248 | tf_op jit(solution)/shard_map/while/body/eval_jaxpr/ppermute | solution.py:15
  201.5 5.3 %conditional.5 = (bf16[3,24,512]{2,1,0:T(8,128)(2,1)S(1)}) conditional(s32[]{:T(128)} %bitcast.46, () %tuple.54, (bf16[2,3,4096]{2,1,0:T(4,128)(2,1)S(1)}, bf16[2,24,4096]{2,1,0:T(8,128)(2,1)S(1)}, bf16[8192,512]{1,0:T(8,128)(2,1)}) %tuple.55), branch_computations={%region_3.3_spmd, %region_4.4_spmd} | conditional | flops 608919552 | bytes 13033480 | solution.py:53
  201.9 5.0 %fusion.8 = bf16[3,24,512]{2,1,0:T(8,128)(2,1)S(1)} fusion(bf16[8192,512]{1,0:T(8,128)(2,1)} %get-tuple-element.141, bf16[3,24,4096]{2,1,0:T(8,128)(2,1)S(1)} %get-tuple-element.205, bf16[3,24,4096]{2,1,0:T(8,128)(2,1)S(1)} %get-tuple-element.204), kind=kOutput, calls=%fused_computation.13 | convolution fusion | flops 606339072 | bytes 9641984 | tf_op jit(solution)/shard_map/while/body/eval_jaxpr/cond/branch_1_fun/dot_general | solution.py:46
  209.0 1.3 dynamic_slice.27
  211.0 5.4 %collective-permute-done = bf16[2,24,4096]{2,1,0:T(8,128)(2,1)S(1)} collective-permute-done((bf16[2,24,4096]{2,1,0:T(8,128)(2,1)S(1)}, bf16[2,24,4096]{2,1,0:T(8,128)(2,1)S(1)}, u32[]{:S(2)}, u32[]{:S(2)}) %collective-permute-start) | collective-permute-done | bytes 393248 | tf_op jit(solution)/shard_map/while/body/eval_jaxpr/ppermute | solution.py:15
  220.6 6.7 %collective-permute-done = bf16[2,24,4096]{2,1,0:T(8,128)(2,1)S(1)} collective-permute-done((bf16[2,24,4096]{2,1,0:T(8,128)(2,1)S(1)}, bf16[2,24,4096]{2,1,0:T(8,128)(2,1)S(1)}, u32[]{:S(2)}, u32[]{:S(2)}) %collective-permute-start) | collective-permute-done | bytes 393248 | tf_op jit(solution)/shard_map/while/body/eval_jaxpr/ppermute | solution.py:15
  227.3 5.3 %conditional.5 = (bf16[3,24,512]{2,1,0:T(8,128)(2,1)S(1)}) conditional(s32[]{:T(128)} %bitcast.46, () %tuple.54, (bf16[2,3,4096]{2,1,0:T(4,128)(2,1)S(1)}, bf16[2,24,4096]{2,1,0:T(8,128)(2,1)S(1)}, bf16[8192,512]{1,0:T(8,128)(2,1)}) %tuple.55), branch_computations={%region_3.3_spmd, %region_4.4_spmd} | conditional | flops 608919552 | bytes 13033480 | solution.py:53
  227.7 5.0 %fusion.8 = bf16[3,24,512]{2,1,0:T(8,128)(2,1)S(1)} fusion(bf16[8192,512]{1,0:T(8,128)(2,1)} %get-tuple-element.141, bf16[3,24,4096]{2,1,0:T(8,128)(2,1)S(1)} %get-tuple-element.205, bf16[3,24,4096]{2,1,0:T(8,128)(2,1)S(1)} %get-tuple-element.204), kind=kOutput, calls=%fused_computation.13 | convolution fusion | flops 606339072 | bytes 9641984 | tf_op jit(solution)/shard_map/while/body/eval_jaxpr/cond/branch_1_fun/dot_general | solution.py:46
  236.8 5.4 %collective-permute-done = bf16[2,24,4096]{2,1,0:T(8,128)(2,1)S(1)} collective-permute-done((bf16[2,24,4096]{2,1,0:T(8,128)(2,1)S(1)}, bf16[2,24,4096]{2,1,0:T(8,128)(2,1)S(1)}, u32[]{:S(2)}, u32[]{:S(2)}) %collective-permute-start) | collective-permute-done | bytes 393248 | tf_op jit(solution)/shard_map/while/body/eval_jaxpr/ppermute | solution.py:15
  242.2 5.3 %conditional.5 = (bf16[3,24,512]{2,1,0:T(8,128)(2,1)S(1)}) conditional(s32[]{:T(128)} %bitcast.46, () %tuple.54, (bf16[2,3,4096]{2,1,0:T(4,128)(2,1)S(1)}, bf16[2,24,4096]{2,1,0:T(8,128)(2,1)S(1)}, bf16[8192,512]{1,0:T(8,128)(2,1)}) %tuple.55), branch_computations={%region_3.3_spmd, %region_4.4_spmd} | conditional | flops 608919552 | bytes 13033480 | solution.py:53
  242.5 5.0 %fusion.8 = bf16[3,24,512]{2,1,0:T(8,128)(2,1)S(1)} fusion(bf16[8192,512]{1,0:T(8,128)(2,1)} %get-tuple-element.141, bf16[3,24,4096]{2,1,0:T(8,128)(2,1)S(1)} %get-tuple-element.205, bf16[3,24,4096]{2,1,0:T(8,128)(2,1)S(1)} %get-tuple-element.204), kind=kOutput, calls=%fused_computation.13 | convolution fusion | flops 606339072 | bytes 9641984 | tf_op jit(solution)/shard_map/while/body/eval_jaxpr/cond/branch_1_fun/dot_general | solution.py:46
  251.7 5.4 %collective-permute-done = bf16[2,24,4096]{2,1,0:T(8,128)(2,1)S(1)} collective-permute-done((bf16[2,24,4096]{2,1,0:T(8,128)(2,1)S(1)}, bf16[2,24,4096]{2,1,0:T(8,128)(2,1)S(1)}, u32[]{:S(2)}, u32[]{:S(2)}) %collective-permute-start) | collective-permute-done | bytes 393248 | tf_op jit(solution)/shard_map/while/body/eval_jaxpr/ppermute | solution.py:15
  257.1 5.3 %conditional.5 = (bf16[3,24,512]{2,1,0:T(8,128)(2,1)S(1)}) conditional(s32[]{:T(128)} %bitcast.46, () %tuple.54, (bf16[2,3,4096]{2,1,0:T(4,128)(2,1)S(1)}, bf16[2,24,4096]{2,1,0:T(8,128)(2,1)S(1)}, bf16[8192,512]{1,0:T(8,128)(2,1)}) %tuple.55), branch_computations={%region_3.3_spmd, %region_4.4_spmd} | conditional | flops 608919552 | bytes 13033480 | solution.py:53
  257.4 5.0 %fusion.8 = bf16[3,24,512]{2,1,0:T(8,128)(2,1)S(1)} fusion(bf16[8192,512]{1,0:T(8,128)(2,1)} %get-tuple-element.141, bf16[3,24,4096]{2,1,0:T(8,128)(2,1)S(1)} %get-tuple-element.205, bf16[3,24,4096]{2,1,0:T(8,128)(2,1)S(1)} %get-tuple-element.204), kind=kOutput, calls=%fused_computation.13 | convolution fusion | flops 606339072 | bytes 9641984 | tf_op jit(solution)/shard_map/while/body/eval_jaxpr/cond/branch_1_fun/dot_general | solution.py:46
  266.5 5.4 %collective-permute-done = bf16[2,24,4096]{2,1,0:T(8,128)(2,1)S(1)} collective-permute-done((bf16[2,24,4096]{2,1,0:T(8,128)(2,1)S(1)}, bf16[2,24,4096]{2,1,0:T(8,128)(2,1)S(1)}, u32[]{:S(2)}, u32[]{:S(2)}) %collective-permute-start) | collective-permute-done | bytes 393248 | tf_op jit(solution)/shard_map/while/body/eval_jaxpr/ppermute | solution.py:15
  271.9 5.3 %conditional.5 = (bf16[3,24,512]{2,1,0:T(8,128)(2,1)S(1)}) conditional(s32[]{:T(128)} %bitcast.46, () %tuple.54, (bf16[2,3,4096]{2,1,0:T(4,128)(2,1)S(1)}, bf16[2,24,4096]{2,1,0:T(8,128)(2,1)S(1)}, bf16[8192,512]{1,0:T(8,128)(2,1)}) %tuple.55), branch_computations={%region_3.3_spmd, %region_4.4_spmd} | conditional | flops 608919552 | bytes 13033480 | solution.py:53
  272.3 5.0 %fusion.8 = bf16[3,24,512]{2,1,0:T(8,128)(2,1)S(1)} fusion(bf16[8192,512]{1,0:T(8,128)(2,1)} %get-tuple-element.141, bf16[3,24,4096]{2,1,0:T(8,128)(2,1)S(1)} %get-tuple-element.205, bf16[3,24,4096]{2,1,0:T(8,128)(2,1)S(1)} %get-tuple-element.204), kind=kOutput, calls=%fused_computation.13 | convolution fusion | flops 606339072 | bytes 9641984 | tf_op jit(solution)/shard_map/while/body/eval_jaxpr/cond/branch_1_fun/dot_general | solution.py:46
  281.4 5.4 %collective-permute-done = bf16[2,24,4096]{2,1,0:T(8,128)(2,1)S(1)} collective-permute-done((bf16[2,24,4096]{2,1,0:T(8,128)(2,1)S(1)}, bf16[2,24,4096]{2,1,0:T(8,128)(2,1)S(1)}, u32[]{:S(2)}, u32[]{:S(2)}) %collective-permute-start) | collective-permute-done | bytes 393248 | tf_op jit(solution)/shard_map/while/body/eval_jaxpr/ppermute | solution.py:15
  (138 shorter events, 28.4 us)
Async XLA Ops:
  79.1 15.3 %collective-permute-start = (bf16[2,24,4096]{2,1,0:T(8,128)(2,1)S(1)}, bf16[2,24,4096]{2,1,0:T(8,128)(2,1)S(1)}, u32[]{:S(2)}, u32[]{:S(2)}) collective-permute-start(bf16[2,24,4096]{2,1,0:T(8,128)(2,1)S(1)} %get-tuple-element.289), channel_id=1, source_target_pairs={{0,248},{8,0},{16,8},{24,16},{32,24},{40,32},{48,40},{56,48},{64,5... | collective-permute-start | bytes 1179656 | tf_op jit(solution)/shard_map/while/body/eval_jaxpr/ppermute | solution.py:15
  99.8 9.4 %collective-permute-start = (bf16[2,24,4096]{2,1,0:T(8,128)(2,1)S(1)}, bf16[2,24,4096]{2,1,0:T(8,128)(2,1)S(1)}, u32[]{:S(2)}, u32[]{:S(2)}) collective-permute-start(bf16[2,24,4096]{2,1,0:T(8,128)(2,1)S(1)} %get-tuple-element.289), channel_id=1, source_target_pairs={{0,248},{8,0},{16,8},{24,16},{32,24},{40,32},{48,40},{56,48},{64,5... | collective-permute-start | bytes 1179656 | tf_op jit(solution)/shard_map/while/body/eval_jaxpr/ppermute | solution.py:15
  109.4 10.7 %collective-permute-start = (bf16[2,24,4096]{2,1,0:T(8,128)(2,1)S(1)}, bf16[2,24,4096]{2,1,0:T(8,128)(2,1)S(1)}, u32[]{:S(2)}, u32[]{:S(2)}) collective-permute-start(bf16[2,24,4096]{2,1,0:T(8,128)(2,1)S(1)} %get-tuple-element.289), channel_id=1, source_target_pairs={{0,248},{8,0},{16,8},{24,16},{32,24},{40,32},{48,40},{56,48},{64,5... | collective-permute-start | bytes 1179656 | tf_op jit(solution)/shard_map/while/body/eval_jaxpr/ppermute | solution.py:15
  120.2 10.7 %collective-permute-start = (bf16[2,24,4096]{2,1,0:T(8,128)(2,1)S(1)}, bf16[2,24,4096]{2,1,0:T(8,128)(2,1)S(1)}, u32[]{:S(2)}, u32[]{:S(2)}) collective-permute-start(bf16[2,24,4096]{2,1,0:T(8,128)(2,1)S(1)} %get-tuple-element.289), channel_id=1, source_target_pairs={{0,248},{8,0},{16,8},{24,16},{32,24},{40,32},{48,40},{56,48},{64,5... | collective-permute-start | bytes 1179656 | tf_op jit(solution)/shard_map/while/body/eval_jaxpr/ppermute | solution.py:15
  136.4 9.4 %collective-permute-start = (bf16[2,24,4096]{2,1,0:T(8,128)(2,1)S(1)}, bf16[2,24,4096]{2,1,0:T(8,128)(2,1)S(1)}, u32[]{:S(2)}, u32[]{:S(2)}) collective-permute-start(bf16[2,24,4096]{2,1,0:T(8,128)(2,1)S(1)} %get-tuple-element.289), channel_id=1, source_target_pairs={{0,248},{8,0},{16,8},{24,16},{32,24},{40,32},{48,40},{56,48},{64,5... | collective-permute-start | bytes 1179656 | tf_op jit(solution)/shard_map/while/body/eval_jaxpr/ppermute | solution.py:15
  151.3 9.4 %collective-permute-start = (bf16[2,24,4096]{2,1,0:T(8,128)(2,1)S(1)}, bf16[2,24,4096]{2,1,0:T(8,128)(2,1)S(1)}, u32[]{:S(2)}, u32[]{:S(2)}) collective-permute-start(bf16[2,24,4096]{2,1,0:T(8,128)(2,1)S(1)} %get-tuple-element.289), channel_id=1, source_target_pairs={{0,248},{8,0},{16,8},{24,16},{32,24},{40,32},{48,40},{56,48},{64,5... | collective-permute-start | bytes 1179656 | tf_op jit(solution)/shard_map/while/body/eval_jaxpr/ppermute | solution.py:15
  160.9 9.4 %collective-permute-start = (bf16[2,24,4096]{2,1,0:T(8,128)(2,1)S(1)}, bf16[2,24,4096]{2,1,0:T(8,128)(2,1)S(1)}, u32[]{:S(2)}, u32[]{:S(2)}) collective-permute-start(bf16[2,24,4096]{2,1,0:T(8,128)(2,1)S(1)} %get-tuple-element.289), channel_id=1, source_target_pairs={{0,248},{8,0},{16,8},{24,16},{32,24},{40,32},{48,40},{56,48},{64,5... | collective-permute-start | bytes 1179656 | tf_op jit(solution)/shard_map/while/body/eval_jaxpr/ppermute | solution.py:15
  170.4 10.7 %collective-permute-start = (bf16[2,24,4096]{2,1,0:T(8,128)(2,1)S(1)}, bf16[2,24,4096]{2,1,0:T(8,128)(2,1)S(1)}, u32[]{:S(2)}, u32[]{:S(2)}) collective-permute-start(bf16[2,24,4096]{2,1,0:T(8,128)(2,1)S(1)} %get-tuple-element.289), channel_id=1, source_target_pairs={{0,248},{8,0},{16,8},{24,16},{32,24},{40,32},{48,40},{56,48},{64,5... | collective-permute-start | bytes 1179656 | tf_op jit(solution)/shard_map/while/body/eval_jaxpr/ppermute | solution.py:15
  181.3 9.4 %collective-permute-start = (bf16[2,24,4096]{2,1,0:T(8,128)(2,1)S(1)}, bf16[2,24,4096]{2,1,0:T(8,128)(2,1)S(1)}, u32[]{:S(2)}, u32[]{:S(2)}) collective-permute-start(bf16[2,24,4096]{2,1,0:T(8,128)(2,1)S(1)} %get-tuple-element.289), channel_id=1, source_target_pairs={{0,248},{8,0},{16,8},{24,16},{32,24},{40,32},{48,40},{56,48},{64,5... | collective-permute-start | bytes 1179656 | tf_op jit(solution)/shard_map/while/body/eval_jaxpr/ppermute | solution.py:15
  190.8 10.7 %collective-permute-start = (bf16[2,24,4096]{2,1,0:T(8,128)(2,1)S(1)}, bf16[2,24,4096]{2,1,0:T(8,128)(2,1)S(1)}, u32[]{:S(2)}, u32[]{:S(2)}) collective-permute-start(bf16[2,24,4096]{2,1,0:T(8,128)(2,1)S(1)} %get-tuple-element.289), channel_id=1, source_target_pairs={{0,248},{8,0},{16,8},{24,16},{32,24},{40,32},{48,40},{56,48},{64,5... | collective-permute-start | bytes 1179656 | tf_op jit(solution)/shard_map/while/body/eval_jaxpr/ppermute | solution.py:15
  207.0 9.4 %collective-permute-start = (bf16[2,24,4096]{2,1,0:T(8,128)(2,1)S(1)}, bf16[2,24,4096]{2,1,0:T(8,128)(2,1)S(1)}, u32[]{:S(2)}, u32[]{:S(2)}) collective-permute-start(bf16[2,24,4096]{2,1,0:T(8,128)(2,1)S(1)} %get-tuple-element.289), channel_id=1, source_target_pairs={{0,248},{8,0},{16,8},{24,16},{32,24},{40,32},{48,40},{56,48},{64,5... | collective-permute-start | bytes 1179656 | tf_op jit(solution)/shard_map/while/body/eval_jaxpr/ppermute | solution.py:15
  216.6 10.7 %collective-permute-start = (bf16[2,24,4096]{2,1,0:T(8,128)(2,1)S(1)}, bf16[2,24,4096]{2,1,0:T(8,128)(2,1)S(1)}, u32[]{:S(2)}, u32[]{:S(2)}) collective-permute-start(bf16[2,24,4096]{2,1,0:T(8,128)(2,1)S(1)} %get-tuple-element.289), channel_id=1, source_target_pairs={{0,248},{8,0},{16,8},{24,16},{32,24},{40,32},{48,40},{56,48},{64,5... | collective-permute-start | bytes 1179656 | tf_op jit(solution)/shard_map/while/body/eval_jaxpr/ppermute | solution.py:15
  232.8 9.4 %collective-permute-start = (bf16[2,24,4096]{2,1,0:T(8,128)(2,1)S(1)}, bf16[2,24,4096]{2,1,0:T(8,128)(2,1)S(1)}, u32[]{:S(2)}, u32[]{:S(2)}) collective-permute-start(bf16[2,24,4096]{2,1,0:T(8,128)(2,1)S(1)} %get-tuple-element.289), channel_id=1, source_target_pairs={{0,248},{8,0},{16,8},{24,16},{32,24},{40,32},{48,40},{56,48},{64,5... | collective-permute-start | bytes 1179656 | tf_op jit(solution)/shard_map/while/body/eval_jaxpr/ppermute | solution.py:15
  247.7 9.4 %collective-permute-start = (bf16[2,24,4096]{2,1,0:T(8,128)(2,1)S(1)}, bf16[2,24,4096]{2,1,0:T(8,128)(2,1)S(1)}, u32[]{:S(2)}, u32[]{:S(2)}) collective-permute-start(bf16[2,24,4096]{2,1,0:T(8,128)(2,1)S(1)} %get-tuple-element.289), channel_id=1, source_target_pairs={{0,248},{8,0},{16,8},{24,16},{32,24},{40,32},{48,40},{56,48},{64,5... | collective-permute-start | bytes 1179656 | tf_op jit(solution)/shard_map/while/body/eval_jaxpr/ppermute | solution.py:15
  262.5 9.4 %collective-permute-start = (bf16[2,24,4096]{2,1,0:T(8,128)(2,1)S(1)}, bf16[2,24,4096]{2,1,0:T(8,128)(2,1)S(1)}, u32[]{:S(2)}, u32[]{:S(2)}) collective-permute-start(bf16[2,24,4096]{2,1,0:T(8,128)(2,1)S(1)} %get-tuple-element.289), channel_id=1, source_target_pairs={{0,248},{8,0},{16,8},{24,16},{32,24},{40,32},{48,40},{56,48},{64,5... | collective-permute-start | bytes 1179656 | tf_op jit(solution)/shard_map/while/body/eval_jaxpr/ppermute | solution.py:15
  277.4 9.4 %collective-permute-start = (bf16[2,24,4096]{2,1,0:T(8,128)(2,1)S(1)}, bf16[2,24,4096]{2,1,0:T(8,128)(2,1)S(1)}, u32[]{:S(2)}, u32[]{:S(2)}) collective-permute-start(bf16[2,24,4096]{2,1,0:T(8,128)(2,1)S(1)} %get-tuple-element.289), channel_id=1, source_target_pairs={{0,248},{8,0},{16,8},{24,16},{32,24},{40,32},{48,40},{56,48},{64,5... | collective-permute-start | bytes 1179656 | tf_op jit(solution)/shard_map/while/body/eval_jaxpr/ppermute | solution.py:15
where the time goes:
time: 290 us; the launch traced here: 288 us
  waiting for transfers between devices  91.9 us (32%)
  other arithmetic  49.5 us (17%)
  matrix products  44.8 us (15%)
  loops' own time  32.5 us (11%)
  local copies, waits for them, and re-layouts  31.6 us (11%)
  blocking collectives  29 us (10%)
  starting transfers between devices  8.14 us (3%)
    ppermute x16, waiting for transfers between devices, shifted(): return lax.ppermute(value, axis, pairs)  91.9 us
    dot_general x9, matrix products, compute(): jnp.dot(product, table, preferred_element_type=jnp.float32)  44.8 us
    another operation x10, other arithmetic  37.9 us
    another operation x1, loops' own time, local(): lax.scan(advance, moving, jnp.arange(1, cycle // 2 + 1, dtype=jnp.int32))[1]  32.3 us
    all_gather x1, blocking collectives, local(): moving = lax.all_gather(spectra, 'freq', axis=2, tiled=True)  29 us
    dynamic_slice x17, local copies, waits for them, and re-layouts, correlate(): flag = pair_mask[block, (block + offset) % cycle]  21.7 us
    dynamic_slice x16, local copies, waits for them, and re-layouts, local(): lax.scan(advance, moving, jnp.arange(1, cycle // 2 + 1, dtype=jnp.int32))[1]  9.42 us
    ppermute x16, starting transfers between devices, shifted(): return lax.ppermute(value, axis, pairs)  8.14 us
  transfers between devices with their start and end apart: 16, of which 16 were waited for; matrix products, arithmetic and copies ran while one was open for 11% of the time, Pallas kernels for 0%

commit v1 on v0

v1 whole, which is shorter than its diff:
```python
import functools
import math

import jax
import jax.numpy as jnp
import ml_dtypes
import numpy as np
from jax import lax
from jax.experimental import pallas as pl
from jax.experimental.pallas import tpu as pltpu
from jax.sharding import PartitionSpec as P

FREQS = 4096
LAGS = 512
HALF = LAGS // 2
STA = 24
BAND = 512
BANDS = 8
OWN = 3
UNITS = 4
PER_UNIT = 4
PAIRS = PER_UNIT * OWN
ROWS = PAIRS * STA
MAIN = 32
LEFT = 4
MESH = pl.DeviceIdType.MESH
F32 = jnp.float32
BF16 = jnp.bfloat16


def half_tables():
    bins = np.arange(FREQS, dtype=np.float64)[:, None]
    lags = np.arange(HALF, dtype=np.float64)[None, :] + 0.5
    angle = math.pi * bins * lags / FREQS
    both = np.concatenate([np.cos(angle), np.sin(angle)], axis=1) / math.sqrt(FREQS)
    return both.astype(np.float32).astype(ml_dtypes.bfloat16).reshape(BANDS, BAND, LAGS)


def phases():
    angle = math.pi * np.arange(FREQS, dtype=np.float64) / (2 * FREQS)
    both = np.stack([np.cos(angle), np.sin(angle)])
    return both.reshape(2 * BANDS, 1, BAND).astype(np.float32)


def piece_select():
    select = np.zeros((4, BANDS * 16, STA), np.float32)
    for dest in range(BANDS):
        for jj in range(OWN):
            for part in range(2):
                for half in range(2):
                    row = dest * 16 + (jj * 2 + part) * 2 + half
                    select[part * 2 + half, row, OWN * dest + jj] = 1
    return select.astype(ml_dtypes.bfloat16)


def send_select():
    select = np.zeros((BANDS * (MAIN + LEFT), ROWS), np.float32)
    for dest in range(BANDS):
        for kk in range(PER_UNIT):
            for il in range(OWN):
                for jj in range(OWN):
                    r = kk * 9 + il * OWN + jj
                    row = dest * MAIN + r if r < MAIN else BANDS * MAIN + dest * LEFT + r - MAIN
                    select[row, (kk * OWN + jj) * STA + OWN * dest + il] = 1
    return select.astype(ml_dtypes.bfloat16)


def left_select():
    select = np.zeros((128, 128), np.float32)
    for unit in range(UNITS):
        for dest in range(BANDS):
            for r in range(LEFT):
                select[dest * 16 + unit * LEFT + r, unit * 32 + dest * LEFT + r] = 1
    return select.astype(ml_dtypes.bfloat16)


def final_select():
    first = np.zeros((216, 256), np.float32)
    last = np.zeros((72, 256), np.float32)
    left = np.zeros((UNITS, 72, 128), np.float32)
    for source in range(BANDS):
        for il in range(OWN):
            for jj in range(OWN):
                row = il * STA + OWN * source + jj
                nine = il * OWN + jj
                for kk in range(3):
                    first[kk * 72 + row, source * MAIN + kk * 9 + nine] = 1
                if nine < 5:
                    last[row, source * MAIN + 27 + nine] = 1
                else:
                    for unit in range(UNITS):
                        left[unit, row, source * 16 + unit * LEFT + nine - 5] = 1
    cast = ml_dtypes.bfloat16
    return first.astype(cast), last.astype(cast), left.astype(cast)


def flip():
    return np.eye(HALF, dtype=np.float32)[::-1].astype(ml_dtypes.bfloat16)


def dot(a, b):
    return jnp.dot(a, b, preferred_element_type=F32)


def kernel(
    x_ref, mask_ref, phase_ref, piece_ref, send_ref, lefts_ref, first_ref, last_ref, left_ref, flip_ref, table_hbm,
    out_ref,
    table, pieces, b_land, a_land, a_spec, b_spec, lre0, lim0, lre1, lim1, acc, prod, s_main, s_lefts, s_left, m_main, m_left,
    table_sem, b_send, b_recv, a_send, a_recv, ring_send, ring_recv, sib_send, sib_recv, o_send, o_recv, l_send, l_recv,
):
    sta, freq = lax.axis_index("sta"), lax.axis_index("freq")
    z, quad = sta // 4, sta % 4
    ylo, core = quad // 2, quad % 2
    xx, yhi = freq // 2, freq % 2

    fetch = pltpu.make_async_copy(table_hbm, table, table_sem)
    fetch.start()

    def peer(dx, dh, dl):
        return (
            z * 4 + (ylo + dl) % 2 * 2 + core,
            (xx + dx) % 4 * 2 + (yhi + dh) % 2,
        )

    plane = [(dx, dh, dl) for dl in range(2) for dh in range(2) for dx in range(4)]
    others = plane[1:]
    group = [d for d in others if d[2] == 0]
    below = ((sta + 28) % 32, freq)
    above = ((sta + 4) % 32, freq)
    sibling = (z * 4 + ylo * 2 + (1 - core), freq)

    barrier = pltpu.get_barrier_semaphore()
    for device in [peer(*d) for d in others] + [sibling, above]:
        pl.semaphore_signal(barrier, inc=1, device_id=device, device_id_type=MESH)

    total = None
    for part in range(2):
        for half in range(2):
            term = dot(piece_ref[part * 2 + half], x_ref[part, :, half * 256 : half * 256 + 256])
            total = term if total is None else total + term
    pieces[...] = total.astype(BF16).reshape(BANDS, 16, 256)

    pl.semaphore_wait(barrier, len(others) + 2)

    def remote(src, dst, send, recv, device):
        return pltpu.make_async_remote_copy(
            src_ref=src, dst_ref=dst, send_sem=send, recv_sem=recv, device_id=device, device_id_type=MESH
        )

    b_copies = []
    for n, d in enumerate(others):
        device = peer(*d)
        b_copies.append(
            remote(pieces.at[device[1]], b_land.at[0, core, ylo, freq], b_send.at[n], b_recv.at[n], device)
        )
    a_copies = []
    for n, d in enumerate(group):
        a_copies.append(remote(x_ref, a_land.at[freq], a_send.at[n], a_recv.at[n], peer(*d)))
    for copy in b_copies + a_copies:
        copy.start()
    b_land[0, core, ylo, freq] = pieces[freq]
    a_land[freq] = x_ref[...]

    def ring(s, part):
        return remote(
            b_land.at[s, core, part], b_land.at[s + 1, core, part], ring_send.at[s, part], ring_recv.at[s, part], below
        )

    def across(s, part):
        return remote(
            b_land.at[s, core, part], b_land.at[s, core, part], sib_send.at[s, part], sib_recv.at[s, part], sibling
        )

    def forward(s):
        for part in range(2):
            if s > 0:
                ring(s - 1, part).wait_recv()
            if s < UNITS:
                ring(s, part).start()
            across(s, part).start()

    for copy in b_copies:
        copy.wait_recv()
    forward(0)

    for copy in a_copies:
        copy.wait_recv()

    def rotate(h, carry):
        cos, sin = phase_ref[h], phase_ref[BANDS + h]
        re = a_land[h, 0].astype(F32)
        im = a_land[h, 1].astype(F32)
        a_spec[h, 0] = re * cos + im * sin
        a_spec[h, 1] = im * cos - re * sin
        return carry

    lax.fori_loop(0, BANDS, rotate, 0)
    fetch.wait()

    def project(buffers, h, rows):
        lre, lim = buffers
        acc[:rows, :HALF] += dot(lre[:rows], table[h, :, :HALF])
        acc[:rows, HALF:] += dot(lim[:rows], table[h, :, HALF:])

    def products(cross, rows):
        acc[:rows] = jnp.zeros((rows, LAGS), F32)
        even, odd = (lre0, lim0), (lre1, lim1)
        cross(0, even)

        def step(i, carry):
            cross(2 * i + 1, odd)
            project(even, 2 * i, rows)
            cross(2 * i + 2, even)
            project(odd, 2 * i + 1, rows)
            return carry

        lax.fori_loop(0, 3, step, 0)
        cross(7, odd)
        project(even, 6, rows)
        project(odd, 7, rows)
        cos, sin = acc[:rows, :HALF], acc[:rows, HALF:]
        return (cos + sin).astype(BF16), (cos - sin).astype(BF16)

    def cross_unit(h, buffers):
        for half in range(2):
            lanes = slice(half * 256, half * 256 + 256)
            ar, ai = a_spec[h, 0, :, lanes], a_spec[h, 1, :, lanes]
            for two in range(PAIRS // 2):
                re, im = [], []
                for g in (2 * two, 2 * two + 1):
                    kk, jj = g // OWN, g % OWN
                    row = jj * 4 + half
                    br = b_spec[h, kk, row : row + 1, :]
                    bi = b_spec[h, kk, row + 2 : row + 3, :]
                    re.append(ar * br + ai * bi)
                    im.append(ai * br - ar * bi)
                buffers[0][two * 48 : two * 48 + 48, lanes] = jnp.concatenate(re, axis=0).astype(BF16)
                buffers[1][two * 48 : two * 48 + 48, lanes] = jnp.concatenate(im, axis=0).astype(BF16)

    def cross_own(h, buffers):
        for half in range(2):
            lanes = slice(half * 256, half * 256 + 256)
            br = a_land[h, 0, :, lanes].astype(F32)
            bi = a_land[h, 1, :, lanes].astype(F32)
            re, im = [], []
            for il in (0, 1, 2, 2):
                ar = a_spec[h, 0, pl.ds(OWN * freq + il, 1), lanes]
                ai = a_spec[h, 1, pl.ds(OWN * freq + il, 1), lanes]
                re.append(ar * br + ai * bi)
                im.append(ai * br - ar * bi)
            buffers[0][:96, lanes] = jnp.concatenate(re, axis=0).astype(BF16)
            buffers[1][:96, lanes] = jnp.concatenate(im, axis=0).astype(BF16)

    def out_copies(unit):
        copies = []
        for n, d in enumerate(group):
            device = peer(*d)
            copies.append(
                remote(s_main.at[unit, device[1]], m_main.at[unit, freq], o_send.at[unit, n], o_recv.at[unit, n], device)
            )
        return copies

    def left_copies():
        copies = []
        for n, d in enumerate(group):
            device = peer(*d)
            copies.append(remote(s_left.at[device[1]], m_left.at[freq], l_send.at[n], l_recv.at[n], device))
        return copies

    def write(offset, value, keep=None):
        on = mask_ref[sta, (sta + offset) % 32] > 0
        value = jnp.where(on, value, 0.0)
        if keep is not None:
            value = jnp.where(keep, value, 0.0)
        out_ref[offset] = value.reshape(OWN, STA, LAGS).astype(BF16)

    def finish(unit):
        for copy in out_copies(unit):
            copy.wait_recv()
        rows = dot(first_ref[...], m_main[unit].reshape(256, LAGS))
        low = dot(rows[:, :HALF].astype(BF16), flip_ref[...])
        rows = jnp.concatenate([low, rows[:, HALF:]], axis=1)
        for kk in range(3):
            write(unit * PER_UNIT + 1 + kk, rows[kk * 72 : kk * 72 + 72])

    for unit in range(UNITS):
        forward(unit + 1)
        for s in ([0, 1] if unit == 0 else [unit + 1]):
            for part in range(2):
                across(s, part).wait_recv()
        for kk in range(PER_UNIT):
            slot = quad + unit * PER_UNIT + 1 + kk
            spot = slot % 4
            b_spec[:, kk] = b_land[slot // 4, spot % 2, spot // 2].astype(F32)
        low, high = products(cross_unit, ROWS)
        prod[:, :HALF] = low
        prod[:, HALF:] = high
        rows = dot(send_ref[...], prod[...])
        s_main[unit] = rows[:256].astype(BF16).reshape(BANDS, MAIN, LAGS)
        s_lefts[unit] = rows[256:].astype(BF16)
        for copy in out_copies(unit):
            copy.start()
        m_main[unit, freq] = s_main[unit, freq]
        if unit > 0:
            finish(unit - 1)

    s_left[...] = dot(lefts_ref[...], s_lefts[...].reshape(128, LAGS)).astype(BF16).reshape(BANDS, 16, LAGS)
    for copy in left_copies():
        copy.start()
    m_left[freq] = s_left[freq]

    low, high = products(cross_own, 96)
    low = dot(low, flip_ref[...])
    value = jnp.concatenate([low, high.astype(F32)], axis=1)[:72]
    row = lax.broadcasted_iota(jnp.int32, (72, LAGS), 0)
    mine = row // STA + OWN * freq
    write(0, value, row % STA != mine)

    finish(UNITS - 1)
    for copy in left_copies():
        copy.wait_recv()
    for unit in range(UNITS):
        rows = dot(last_ref[...], m_main[unit].reshape(256, LAGS)) + dot(left_ref[unit], m_left[...].reshape(128, LAGS))
        low = dot(rows[:, :HALF].astype(BF16), flip_ref[...])
        write(unit * PER_UNIT + 4, jnp.concatenate([low, rows[:, HALF:]], axis=1))

    for copy in b_copies + a_copies + left_copies():
        copy.wait_send()
    for unit in range(UNITS):
        for copy in out_copies(unit):
            copy.wait_send()
        for part in range(2):
            ring(unit, part).wait_send()
    for s in range(UNITS + 1):
        for part in range(2):
            across(s, part).wait_send()


def local(spectra, pair_mask):
    first, last, left = final_select()
    small = [phases(), piece_select(), send_select(), left_select(), first, last, left, flip()]
    vmem = pl.BlockSpec(memory_space=pltpu.VMEM)
    dma = pltpu.SemaphoreType.DMA
    out = pl.pallas_call(
        kernel,
        out_shape=jax.ShapeDtypeStruct((17, OWN, STA, LAGS), BF16),
        in_specs=[vmem, pl.BlockSpec(memory_space=pltpu.SMEM)] + [vmem] * len(small) + [pl.BlockSpec(memory_space=pl.ANY)],
        out_specs=vmem,
        scratch_shapes=[
            pltpu.VMEM((BANDS, BAND, LAGS), BF16),
            pltpu.VMEM((BANDS, 16, 256), BF16),
            pltpu.VMEM((UNITS + 1, 2, 2, BANDS, 16, 256), BF16),
            pltpu.VMEM((BANDS, 2, STA, BAND), BF16),
            pltpu.VMEM((BANDS, 2, STA, BAND), F32),
            pltpu.VMEM((BANDS, PER_UNIT, 16, 256), F32),
            pltpu.VMEM((ROWS, BAND), BF16),
            pltpu.VMEM((ROWS, BAND), BF16),
            pltpu.VMEM((ROWS, BAND), BF16),
            pltpu.VMEM((ROWS, BAND), BF16),
            pltpu.VMEM((ROWS, LAGS), F32),
            pltpu.VMEM((ROWS, LAGS), BF16),
            pltpu.VMEM((UNITS, BANDS, MAIN, LAGS), BF16),
            pltpu.VMEM((UNITS, BANDS * LEFT, LAGS), BF16),
            pltpu.VMEM((BANDS, 16, LAGS), BF16),
            pltpu.VMEM((UNITS, BANDS, MAIN, LAGS), BF16),
            pltpu.VMEM((BANDS, 16, LAGS), BF16),
            dma,
            dma((15,)),
            dma((15,)),
            dma((7,)),
            dma((7,)),
            dma((UNITS, 2)),
            dma((UNITS, 2)),
            dma((UNITS + 1, 2)),
            dma((UNITS + 1, 2)),
            dma((UNITS, 7)),
            dma((UNITS, 7)),
            dma((7,)),
            dma((7,)),
        ],
        compiler_params=pltpu.CompilerParams(
            collective_id=0, has_side_effects=True, vmem_limit_bytes=48 * 1024 * 1024
        ),
        cost_estimate=pl.CostEstimate(flops=10_000_000_000, bytes_accessed=8_000_000, transcendentals=0),
        name="correlate",
    )(spectra, pair_mask, *[jnp.asarray(value) for value in small], jnp.asarray(half_tables()))
    return out[None]


def solution(mesh):
    return jax.shard_map(
        local,
        mesh=mesh,
        in_specs=(P(None, "sta", "freq"), P()),
        out_specs=P("sta", None, "freq", None, None),
        check_vma=False,
    )
```

time: 290 us -> 57.3 us (0.20)
  the two profiles are of different devices: /device:TPU:121 before, /device:TPU:65 now
where the time goes in v1:
time: 57.3 us; the launch traced here: 56.8 us
  Pallas kernels  47.4 us (83%)
  local copies, waits for them, and re-layouts  9.36 us (16%)
    pallas_call x1, Pallas kernels, local(): pl.pallas_call(kernel, out_shape=jax.ShapeDtypeStruct((17, OWN, STA, LAGS...  47.4 us
    unnamed x21, local copies, waits for them, and re-layouts  9.36 us

profile of v1, /device:TPU:65, one launch (start us, length us, event | category | flops | bytes accessed | tf_op | source)
XLA Modules:
  0.0 56.8 jit_solution(14442402845344618877)
XLA Ops:
  0.0 0.0 copy-start
  0.0 0.8 %copy-done = bf16[2,24,512]{2,1,0:T(8,128)(2,1)S(1)} copy-done((bf16[2,24,512]{2,1,0:T(8,128)(2,1)S(1)}, bf16[2,24,512]{2,1,0:T(8,128)(2,1)}, u32[]{:S(2)}) %copy-start) | copy-done | bytes 49176
  0.8 0.0 copy-start.1
  0.8 0.7 %copy-done.1 = s32[32,32]{1,0:T(8,128)S(1)} copy-done((s32[32,32]{1,0:T(8,128)S(1)}, s32[32,32]{1,0:T(8,128)}, u32[]{:S(2)}) %copy-start.1) | copy-done | bytes 4120
  1.5 0.0 copy-start.2
  1.5 0.9 %copy-done.2 = bf16[288,288]{1,0:T(8,128)(2,1)S(1)} copy-done((bf16[288,288]{1,0:T(8,128)(2,1)S(1)}, bf16[288,288]{1,0:T(8,128)(2,1)}, u32[]{:S(2)}) %copy-start.2) | copy-done | bytes 165912
  2.5 0.0 copy-start.3
  2.5 0.9 %copy-done.3 = bf16[256,256]{1,0:T(8,128)(2,1)S(1)} copy-done((bf16[256,256]{1,0:T(8,128)(2,1)S(1)}, bf16[256,256]{1,0:T(8,128)(2,1)}, u32[]{:S(2)}) %copy-start.3) | copy-done | bytes 131096
  3.4 0.0 copy-start.4
  3.4 0.9 %copy-done.4 = bf16[4,128,24]{2,1,0:T(8,128)(2,1)S(1)} copy-done((bf16[4,128,24]{2,1,0:T(8,128)(2,1)S(1)}, bf16[4,128,24]{2,1,0:T(8,128)(2,1)}, u32[]{:S(2)}) %copy-start.4) | copy-done | bytes 24600
  4.3 0.0 copy-start.5
  4.3 0.9 %copy-done.5 = bf16[216,256]{1,0:T(8,128)(2,1)S(1)} copy-done((bf16[216,256]{1,0:T(8,128)(2,1)S(1)}, bf16[216,256]{1,0:T(8,128)(2,1)}, u32[]{:S(2)}) %copy-start.5) | copy-done | bytes 110616
  5.2 0.0 copy-start.6
  5.2 0.9 %copy-done.6 = bf16[4,72,128]{2,1,0:T(8,128)(2,1)S(1)} copy-done((bf16[4,72,128]{2,1,0:T(8,128)(2,1)S(1)}, bf16[4,72,128]{2,1,0:T(8,128)(2,1)}, u32[]{:S(2)}) %copy-start.6) | copy-done | bytes 73752
  6.0 0.0 copy-start.7
  6.0 0.8 %copy-done.7 = bf16[72,256]{1,0:T(8,128)(2,1)S(1)} copy-done((bf16[72,256]{1,0:T(8,128)(2,1)S(1)}, bf16[72,256]{1,0:T(8,128)(2,1)}, u32[]{:S(2)}) %copy-start.7) | copy-done | bytes 36888
  6.8 0.0 copy-start.8
  6.8 0.8 %copy-done.8 = bf16[128,128]{1,0:T(8,128)(2,1)S(1)} copy-done((bf16[128,128]{1,0:T(8,128)(2,1)S(1)}, bf16[128,128]{1,0:T(8,128)(2,1)}, u32[]{:S(2)}) %copy-start.8) | copy-done | bytes 32792
  7.6 0.0 copy-start.9
  7.6 0.8 %copy-done.9 = f32[16,1,512]{2,1,0:T(1,128)S(1)} copy-done((f32[16,1,512]{2,1,0:T(1,128)S(1)}, f32[16,1,512]{2,1,0:T(1,128)}, u32[]{:S(2)}) %copy-start.9) | copy-done | bytes 32792
  8.3 47.4 %correlate.1 = bf16[17,3,24,512]{3,2,1,0:T(8,128)(2,1)S(1)} custom-call(bf16[2,24,512]{2,1,0:T(8,128)(2,1)S(1)} %copy-done, s32[32,32]{1,0:T(8,128)S(1)} %copy-done.1, f32[16,1,512]{2,1,0:T(1,128)S(1)} %copy-done.9, bf16[4,128,24]{2,1,0:T(8,128)(2,1)S(1)} %copy-done.4, bf16[288,288]{1,0:T(8,128)(2,1)S(1)} %copy-done.2, bf16[128,128]{1,0:T(8,128)(2,1)S(1)} %copy-done.8, ...), custom_call_target="tpu_custom_call" | custom-call | flops 10000000000 | bytes 8000000 | tf_op jit(solution)/shard_map/correlate/pallas_call | solution.py:344
  55.7 1.0 %copy.13 = bf16[1,17,3,24,512]{4,3,2,1,0:T(8,128)(2,1)} copy(bf16[1,17,3,24,512]{4,3,2,1,0:T(8,128)(2,1)S(1)} %bitcast.1) | data formatting | bytes 2506752
Async XLA Ops:
  0.0 0.8 %copy-start = (bf16[2,24,512]{2,1,0:T(8,128)(2,1)S(1)}, bf16[2,24,512]{2,1,0:T(8,128)(2,1)}, u32[]{:S(2)}) copy-start(bf16[2,24,512]{2,1,0:T(8,128)(2,1)} %x_ref.1) | copy-start | bytes 147460
  0.8 0.7 %copy-start.1 = (s32[32,32]{1,0:T(8,128)S(1)}, s32[32,32]{1,0:T(8,128)}, u32[]{:S(2)}) copy-start(s32[32,32]{1,0:T(8,128)} %mask_ref.1) | copy-start | bytes 12292
  1.5 0.9 %copy-start.2 = (bf16[288,288]{1,0:T(8,128)(2,1)S(1)}, bf16[288,288]{1,0:T(8,128)(2,1)}, u32[]{:S(2)}) copy-start(bf16[288,288]{1,0:T(8,128)(2,1)} %constant.20.clone.send_ref) | copy-start | bytes 497668
  2.5 0.9 %copy-start.3 = (bf16[256,256]{1,0:T(8,128)(2,1)S(1)}, bf16[256,256]{1,0:T(8,128)(2,1)}, u32[]{:S(2)}) copy-start(bf16[256,256]{1,0:T(8,128)(2,1)} %constant.25.clone.flip_ref) | copy-start | bytes 393220
  3.4 0.9 %copy-start.4 = (bf16[4,128,24]{2,1,0:T(8,128)(2,1)S(1)}, bf16[4,128,24]{2,1,0:T(8,128)(2,1)}, u32[]{:S(2)}) copy-start(bf16[4,128,24]{2,1,0:T(8,128)(2,1)} %constant.19.clone.piece_ref) | copy-start | bytes 73732
  4.3 0.9 %copy-start.5 = (bf16[216,256]{1,0:T(8,128)(2,1)S(1)}, bf16[216,256]{1,0:T(8,128)(2,1)}, u32[]{:S(2)}) copy-start(bf16[216,256]{1,0:T(8,128)(2,1)} %constant.22.clone.first_ref) | copy-start | bytes 331780
  5.2 0.9 %copy-start.6 = (bf16[4,72,128]{2,1,0:T(8,128)(2,1)S(1)}, bf16[4,72,128]{2,1,0:T(8,128)(2,1)}, u32[]{:S(2)}) copy-start(bf16[4,72,128]{2,1,0:T(8,128)(2,1)} %constant.24.clone.left_ref) | copy-start | bytes 221188
  6.0 0.8 %copy-start.7 = (bf16[72,256]{1,0:T(8,128)(2,1)S(1)}, bf16[72,256]{1,0:T(8,128)(2,1)}, u32[]{:S(2)}) copy-start(bf16[72,256]{1,0:T(8,128)(2,1)} %constant.23.clone.last_ref) | copy-start | bytes 110596
  6.8 0.8 %copy-start.8 = (bf16[128,128]{1,0:T(8,128)(2,1)S(1)}, bf16[128,128]{1,0:T(8,128)(2,1)}, u32[]{:S(2)}) copy-start(bf16[128,128]{1,0:T(8,128)(2,1)} %constant.21.clone.lefts_ref) | copy-start | bytes 98308
  7.6 0.8 %copy-start.9 = (f32[16,1,512]{2,1,0:T(1,128)S(1)}, f32[16,1,512]{2,1,0:T(1,128)}, u32[]{:S(2)}) copy-start(f32[16,1,512]{2,1,0:T(1,128)} %constant.18.clone.phase_ref) | copy-start | bytes 98308

commit v2 on v1

v2 whole, which is shorter than its diff:
```python
import functools
import math

import jax
import jax.numpy as jnp
import ml_dtypes
import numpy as np
from jax import lax
from jax.experimental import pallas as pl
from jax.experimental.pallas import tpu as pltpu
from jax.sharding import PartitionSpec as P

FREQS = 4096
LAGS = 512
HALF = LAGS // 2
STA = 24
BAND = 512
BANDS = 8
OWN = 3
UNITS = 4
PER_UNIT = 4
PAIRS = PER_UNIT * OWN
ROWS = PAIRS * STA
MAIN = 32
LEFT = 4
WIDE = 2 * LAGS + 128
INPUTS = 6
PARTS = 4
MESH = pl.DeviceIdType.MESH
F32 = jnp.float32
BF16 = jnp.bfloat16


def half_tables():
    bins = np.arange(FREQS, dtype=np.float64)[:, None]
    lags = np.arange(HALF, dtype=np.float64)[None, :] + 0.5
    angle = math.pi * bins * lags / FREQS
    both = np.concatenate([np.cos(angle), np.sin(angle)], axis=1) / math.sqrt(FREQS)
    return both.astype(np.float32).astype(ml_dtypes.bfloat16).reshape(BANDS, BAND, LAGS)


def padded(value):
    return np.pad(value, [(0, 0)] * (value.ndim - 2) + [(0, 8), (0, 0)])


def phases():
    angle = math.pi * np.arange(FREQS, dtype=np.float64) / (2 * FREQS)
    both = np.stack([np.cos(angle), np.sin(angle)])
    return both.reshape(2 * BANDS, 1, BAND).astype(np.float32)


def piece_select():
    select = np.zeros((4, BANDS * 16, STA), np.float32)
    for dest in range(BANDS):
        for jj in range(OWN):
            for part in range(2):
                for half in range(2):
                    row = dest * 16 + (jj * 2 + part) * 2 + half
                    select[part * 2 + half, row, OWN * dest + jj] = 1
    return select.astype(ml_dtypes.bfloat16)


def send_select():
    select = np.zeros((BANDS * (MAIN + 16), ROWS), np.float32)
    for dest in range(BANDS):
        for kk in range(PER_UNIT):
            for il in range(OWN):
                for jj in range(OWN):
                    r = kk * 9 + il * OWN + jj
                    column = (kk * OWN + jj) * STA + OWN * dest + il
                    if r < MAIN:
                        select[dest * MAIN + r, column] = 1
                    else:
                        for tile in range(4):
                            select[BANDS * MAIN + dest * 16 + tile * LEFT + r - MAIN, column] = 1
    return select.astype(ml_dtypes.bfloat16)


def final_select():
    main = np.zeros((ROWS, BANDS * MAIN), np.float32)
    left = np.zeros((4 * 72, BANDS * 16), np.float32)
    for source in range(BANDS):
        for kk in range(PER_UNIT):
            for il in range(OWN):
                for jj in range(OWN):
                    r = kk * 9 + il * OWN + jj
                    row = il * STA + OWN * source + jj
                    if r < MAIN:
                        main[kk * 72 + row, r // 16 * 128 + source * 16 + r % 16] = 1
                    else:
                        for tile in range(4):
                            left[tile * 72 + row, source * 16 + tile * LEFT + r - MAIN] = 1
    return main.astype(ml_dtypes.bfloat16), left.astype(ml_dtypes.bfloat16)


def flip():
    return np.eye(HALF, dtype=np.float32)[::-1].astype(ml_dtypes.bfloat16)


def dot(a, b):
    return jnp.dot(a, b, preferred_element_type=F32)


def kernel(
    *refs,
):
    inputs, m_out, own_out, refs = refs[:INPUTS], refs[INPUTS], refs[INPUTS + 1], refs[INPUTS + 2 :]
    held, refs = refs[:INPUTS], refs[INPUTS:]
    x_ref, piece_ref, phase_ref, table, send_ref, flip_ref = held
    (
    pieces, b_land, a_land, a_spec, b_spec, lre0, lim0, lre1, lim1, acc, prod, s_main, own,
    in_sem, b_send, b_recv, a_send, a_recv, ring_send, ring_recv, sib_send, sib_recv, o_send, o_recv, m_sem, own_sem,
    ) = refs
    sta, freq = lax.axis_index("sta"), lax.axis_index("freq")
    z, quad = sta // 4, sta % 4
    ylo, core = quad // 2, quad % 2
    xx, yhi = freq // 2, freq % 2

    fetches = [pltpu.make_async_copy(inputs[n], held[n], in_sem.at[n]) for n in range(INPUTS)]
    for fetch in fetches:
        fetch.start()

    def peer(dx, dh, dl, dz=0):
        return (
            (z + 8 - dz) % 8 * 4 + (ylo + dl) % 2 * 2 + core,
            (xx + dx) % 4 * 2 + (yhi + dh) % 2,
        )

    plane = [(dx, dh, dl) for dl in range(2) for dh in range(2) for dx in range(4)]
    others = plane[1:]
    group = [d for d in others if d[2] == 0]
    below = ((sta + 28) % 32, freq)
    nearby = [(*d, 0) for d in others] + [(*d, 1) for d in plane]
    sibling = (z * 4 + ylo * 2 + (1 - core), freq)

    barrier = pltpu.get_barrier_semaphore()
    for device in [peer(dx, dh, dl, -dz) for dx, dh, dl, dz in nearby] + [sibling]:
        pl.semaphore_signal(barrier, inc=1, device_id=device, device_id_type=MESH)

    fetches[0].wait()
    fetches[1].wait()
    total = None
    for part in range(2):
        for half in range(2):
            term = dot(piece_ref[part * 2 + half, :128], x_ref[part, :, half * 256 : half * 256 + 256])
            total = term if total is None else total + term
    pieces[...] = total.astype(BF16).reshape(BANDS, 16, 256)

    pl.semaphore_wait(barrier, len(nearby) + 1)

    def remote(src, dst, send, recv, device):
        return pltpu.make_async_remote_copy(
            src_ref=src, dst_ref=dst, send_sem=send, recv_sem=recv, device_id=device, device_id_type=MESH
        )

    b_copies = []
    for n, d in enumerate(nearby):
        device = peer(*d)
        b_copies.append(
            remote(pieces.at[device[1]], b_land.at[d[3], core, ylo, freq], b_send.at[n], b_recv.at[n], device)
        )
    a_copies = []
    for n, d in enumerate(group):
        a_copies.append(remote(x_ref, a_land.at[freq], a_send.at[n], a_recv.at[n], peer(*d)))
    for copy in b_copies + a_copies:
        copy.start()
    b_land[0, core, ylo, freq] = pieces[freq]
    a_land[freq] = x_ref[...]

    def ring(s, part):
        y, h = part // 2, pl.ds(part % 2 * 4, 4)
        return remote(
            b_land.at[s, core, y, h], b_land.at[s + 1, core, y, h], ring_send.at[s, part], ring_recv.at[s, part], below
        )

    def across(s, part):
        y, h = part // 2, pl.ds(part % 2 * 4, 4)
        return remote(
            b_land.at[s, core, y, h], b_land.at[s, core, y, h], sib_send.at[s, part], sib_recv.at[s, part], sibling
        )

    def forward(s):
        for part in range(PARTS):
            if s > 1:
                ring(s - 1, part).wait_recv()
            if 0 < s < UNITS:
                ring(s, part).start()
            across(s, part).start()

    for copy in b_copies:
        copy.wait_recv()
    forward(1)
    forward(0)

    for copy in a_copies:
        copy.wait_recv()

    def rotate(h, carry):
        cos, sin = phase_ref[h], phase_ref[BANDS + h]
        re = a_land[h, 0].astype(F32)
        im = a_land[h, 1].astype(F32)
        a_spec[h, 0] = re * cos + im * sin
        a_spec[h, 1] = im * cos - re * sin
        return carry

    fetches[2].wait()
    lax.fori_loop(0, BANDS, rotate, 0)
    for fetch in fetches[3:]:
        fetch.wait()

    def project(buffers, h, rows):
        lre, lim = buffers
        acc[:rows, :HALF] += dot(lre[:rows], table[h, :BAND, :HALF])
        acc[:rows, HALF:] += dot(lim[:rows], table[h, :BAND, HALF:])

    def products(cross, rows):
        acc[:rows] = jnp.zeros((rows, LAGS), F32)
        even, odd = (lre0, lim0), (lre1, lim1)
        cross(0, even)

        def step(i, carry):
            cross(2 * i + 1, odd)
            project(even, 2 * i, rows)
            cross(2 * i + 2, even)
            project(odd, 2 * i + 1, rows)
            return carry

        lax.fori_loop(0, 3, step, 0)
        cross(7, odd)
        project(even, 6, rows)
        project(odd, 7, rows)
        cos, sin = acc[:rows, :HALF], acc[:rows, HALF:]
        return (cos + sin).astype(BF16), (cos - sin).astype(BF16)

    def cross_unit(h, buffers):
        for half in range(2):
            lanes = slice(half * 256, half * 256 + 256)
            ar, ai = a_spec[h, 0, :, lanes], a_spec[h, 1, :, lanes]
            for two in range(PAIRS // 2):
                re, im = [], []
                for g in (2 * two, 2 * two + 1):
                    kk, jj = g // OWN, g % OWN
                    row = jj * 4 + half
                    br = b_spec[h, kk, row : row + 1, :]
                    bi = b_spec[h, kk, row + 2 : row + 3, :]
                    re.append(ar * br + ai * bi)
                    im.append(ai * br - ar * bi)
                buffers[0][two * 48 : two * 48 + 48, lanes] = jnp.concatenate(re, axis=0).astype(BF16)
                buffers[1][two * 48 : two * 48 + 48, lanes] = jnp.concatenate(im, axis=0).astype(BF16)

    def cross_own(h, buffers):
        for half in range(2):
            lanes = slice(half * 256, half * 256 + 256)
            br = a_land[h, 0, :, lanes].astype(F32)
            bi = a_land[h, 1, :, lanes].astype(F32)
            re, im = [], []
            for il in (0, 1, 2, 2):
                ar = a_spec[h, 0, pl.ds(OWN * freq + il, 1), lanes]
                ai = a_spec[h, 1, pl.ds(OWN * freq + il, 1), lanes]
                re.append(ar * br + ai * bi)
                im.append(ai * br - ar * bi)
            buffers[0][:96, lanes] = jnp.concatenate(re, axis=0).astype(BF16)
            buffers[1][:96, lanes] = jnp.concatenate(im, axis=0).astype(BF16)

    def out_copies(unit):
        copies = []
        for n, d in enumerate(group):
            device = peer(*d)
            copies.append(
                remote(s_main.at[unit, device[1]], m_out.at[unit, freq], o_send.at[unit, n], o_recv.at[unit, n], device)
            )
        return copies

    def kept(unit):
        return pltpu.make_async_copy(s_main.at[unit, freq], m_out.at[unit, freq], m_sem.at[unit])

    tile = lax.broadcasted_iota(jnp.int32, (BANDS * 16, 128), 0) // LEFT % 4

    for unit in range(UNITS):
        if unit + 2 <= UNITS:
            forward(unit + 2)
        for s in ([0, 1] if unit == 0 else [unit + 1]):
            for part in range(PARTS):
                across(s, part).wait_recv()
        for kk in range(PER_UNIT):
            slot = quad + unit * PER_UNIT + 1 + kk
            spot = slot % 4
            b_spec[:, kk] = b_land[slot // 4, spot % 2, spot // 2].astype(F32)
        low, high = products(cross_unit, ROWS)
        prod[:, :HALF] = dot(low, flip_ref[:HALF]).astype(BF16)
        prod[:, HALF:] = high
        rows = dot(send_ref[: BANDS * (MAIN + 16)], prod[...])
        main = rows[: BANDS * MAIN].astype(BF16).reshape(BANDS, 2, 16, LAGS)
        s_main[unit, :, :, :LAGS] = main[:, 0]
        s_main[unit, :, :, LAGS : 2 * LAGS] = main[:, 1]
        rows = rows[BANDS * MAIN :]
        left = rows[:, :128]
        for t in range(1, 4):
            left = jnp.where(tile == t, rows[:, t * 128 : t * 128 + 128], left)
        s_main[unit, :, :, 2 * LAGS :] = left.astype(BF16).reshape(BANDS, 16, 128)
        for copy in out_copies(unit):
            copy.start()
        kept(unit).start()

    low, high = products(cross_own, 96)
    low = dot(low, flip_ref[:HALF])
    value = jnp.concatenate([low, high.astype(F32)], axis=1)[:72]
    row = lax.broadcasted_iota(jnp.int32, (72, LAGS), 0)
    mine = row // STA + OWN * freq
    own[...] = jnp.where(row % STA != mine, value, 0.0).reshape(OWN, STA, LAGS).astype(BF16)
    own_copy = pltpu.make_async_copy(own, own_out, own_sem)
    own_copy.start()

    for unit in range(UNITS):
        for copy in out_copies(unit):
            copy.wait_recv()
        kept(unit).wait()
    own_copy.wait()
    for copy in b_copies + a_copies:
        copy.wait_send()
    for unit in range(UNITS):
        for copy in out_copies(unit):
            copy.wait_send()
        if unit > 0:
            for part in range(PARTS):
                ring(unit, part).wait_send()
    for s in range(UNITS + 1):
        for part in range(PARTS):
            across(s, part).wait_send()


def assemble(m_hbm, own_hbm, mask_hbm, main_hbm, left_hbm, out_hbm, m, mask, main_ref, left_ref, done, in_sem, out_sem):
    sta = lax.axis_index("sta")
    sources = [main_hbm, left_hbm, mask_hbm] + [m_hbm.at[unit] for unit in range(UNITS)]
    targets = [main_ref, left_ref, mask] + [m.at[unit] for unit in range(UNITS)]
    fetches = [pltpu.make_async_copy(a, b, in_sem.at[n]) for n, (a, b) in enumerate(zip(sources, targets))]
    for fetch in fetches:
        fetch.start()
    stores = [pltpu.make_async_copy(own_hbm, out_hbm.at[0], out_sem.at[UNITS])]
    stores[0].start()
    for fetch in fetches[:3]:
        fetch.wait()
    for unit in range(UNITS):
        fetches[3 + unit].wait()
        halves = [m[unit, :, :, half * LAGS : half * LAGS + LAGS].reshape(BANDS * 16, LAGS) for half in range(2)]
        rows = dot(main_ref[:ROWS], jnp.concatenate(halves, axis=0))
        left = dot(left_ref[: 4 * 72], m[unit, :, :, 2 * LAGS :].reshape(BANDS * 16, 128))
        left = jnp.concatenate([left[t * 72 : t * 72 + 72] for t in range(4)], axis=1)
        for kk in range(PER_UNIT):
            value = rows[kk * 72 : kk * 72 + 72]
            if kk == PER_UNIT - 1:
                value = value + left
            on = mask[sta, (sta + unit * PER_UNIT + 1 + kk) % 32] > 0
            done[unit, kk] = jnp.where(on, value, 0.0).reshape(OWN, STA, LAGS).astype(BF16)
        store = pltpu.make_async_copy(done.at[unit], out_hbm.at[pl.ds(1 + unit * PER_UNIT, PER_UNIT)], out_sem.at[unit])
        store.start()
        stores.append(store)
    for store in stores:
        store.wait()


def local(spectra, pair_mask):
    main, left = final_select()
    arrays = [spectra, padded(piece_select()), phases(), padded(half_tables()), padded(send_select()), padded(flip())]
    dma = pltpu.SemaphoreType.DMA
    anywhere = pl.BlockSpec(memory_space=pl.ANY)
    held, own = pl.pallas_call(
        kernel,
        out_shape=[
            jax.ShapeDtypeStruct((UNITS, BANDS, 16, WIDE), BF16),
            jax.ShapeDtypeStruct((OWN, STA, LAGS), BF16),
        ],
        in_specs=[anywhere] * INPUTS,
        out_specs=[anywhere] * 2,
        scratch_shapes=[
            *[pltpu.VMEM(value.shape, value.dtype) for value in arrays],
            pltpu.VMEM((BANDS, 16, 256), BF16),
            pltpu.VMEM((UNITS + 1, 2, 2, BANDS, 16, 256), BF16),
            pltpu.VMEM((BANDS, 2, STA, BAND), BF16),
            pltpu.VMEM((BANDS, 2, STA, BAND), F32),
            pltpu.VMEM((BANDS, PER_UNIT, 16, 256), F32),
            pltpu.VMEM((ROWS, BAND), BF16),
            pltpu.VMEM((ROWS, BAND), BF16),
            pltpu.VMEM((ROWS, BAND), BF16),
            pltpu.VMEM((ROWS, BAND), BF16),
            pltpu.VMEM((ROWS, LAGS), F32),
            pltpu.VMEM((ROWS, LAGS), BF16),
            pltpu.VMEM((UNITS, BANDS, 16, WIDE), BF16),
            pltpu.VMEM((OWN, STA, LAGS), BF16),
            dma((INPUTS,)),
            dma((31,)),
            dma((31,)),
            dma((7,)),
            dma((7,)),
            dma((UNITS, PARTS)),
            dma((UNITS, PARTS)),
            dma((UNITS + 1, PARTS)),
            dma((UNITS + 1, PARTS)),
            dma((UNITS, 7)),
            dma((UNITS, 7)),
            dma((UNITS,)),
            dma,
        ],
        compiler_params=pltpu.CompilerParams(
            collective_id=0, has_side_effects=True, vmem_limit_bytes=60 * 1024 * 1024
        ),
        cost_estimate=pl.CostEstimate(flops=10_000_000_000, bytes_accessed=8_000_000, transcendentals=0),
        name="correlate",
    )(*[jnp.asarray(value) for value in arrays])
    selects = [padded(main), padded(left)]
    out = pl.pallas_call(
        assemble,
        out_shape=jax.ShapeDtypeStruct((17, OWN, STA, LAGS), BF16),
        in_specs=[anywhere] * 5,
        out_specs=anywhere,
        scratch_shapes=[
            pltpu.VMEM((UNITS, BANDS, 16, WIDE), BF16),
            pltpu.SMEM(pair_mask.shape, jnp.int32),
            *[pltpu.VMEM(value.shape, value.dtype) for value in selects],
            pltpu.VMEM((UNITS, PER_UNIT, OWN, STA, LAGS), BF16),
            dma((3 + UNITS,)),
            dma((UNITS + 1,)),
        ],
        compiler_params=pltpu.CompilerParams(vmem_limit_bytes=60 * 1024 * 1024),
        cost_estimate=pl.CostEstimate(flops=1_000_000_000, bytes_accessed=4_000_000, transcendentals=0),
        name="assemble",
    )(held, own, pair_mask, *[jnp.asarray(value) for value in selects])
    return out[None]


def solution(mesh):
    return jax.shard_map(
        local,
        mesh=mesh,
        in_specs=(P(None, "sta", "freq"), P()),
        out_specs=P("sta", None, "freq", None, None),
        check_vma=False,
    )
```

time: 57.3 us -> 45 us (0.79)
  the two profiles are of different devices: /device:TPU:65 before, /device:TPU:32 now
where the time goes in v2:
time: 45 us; the launch traced here: 44.7 us
  Pallas kernels  44.7 us (99%)
    pallas_call x1, Pallas kernels, local(): pl.pallas_call(kernel, out_shape=[jax.ShapeDtypeStruct((UNITS, BANDS, 16,...  41.3 us
    pallas_call x1, Pallas kernels, local(): pl.pallas_call(assemble, out_shape=jax.ShapeDtypeStruct((17, OWN, STA, LA...  3.46 us

profile of v2, /device:TPU:32, one launch (start us, length us, event | category | flops | bytes accessed | tf_op | source)
XLA Modules:
  0.0 44.7 jit_solution(1631224962239877129)
XLA Ops:
  0.0 41.3 %correlate.1 = (bf16[4,8,16,1152]{3,2,1,0:T(8,128)(2,1)}, bf16[3,24,512]{2,1,0:T(8,128)(2,1)}) custom-call(bf16[2,24,512]{2,1,0:T(8,128)(2,1)} %refs_0_.1, bf16[4,136,24]{2,1,0:T(8,128)(2,1)} %constant.14.clone.refs_1_, f32[16,1,512]{2,1,0:T(1,128)} %constant.15.clone.refs_2_, bf16[8,520,512]{2,1,0:T(8,128)(2,1)} %constant.16.clone.refs_3_, ...), custom_call_target="tpu_custom_call" | custom-call | flops 10000000000 | bytes 8000000 | tf_op jit(solution)/shard_map/correlate/pallas_call | solution.py:367
  41.3 3.5 %assemble.1 = bf16[17,3,24,512]{3,2,1,0:T(8,128)(2,1)} custom-call(bf16[4,8,16,1152]{3,2,1,0:T(8,128)(2,1)} %get-tuple-element.7.m_hbm, bf16[3,24,512]{2,1,0:T(8,128)(2,1)} %get-tuple-element.8.own_hbm, s32[32,32]{1,0:T(8,128)} %mask_hbm.1, bf16[296,256]{1,0:T(8,128)(2,1)} %constant.19.clone.main_hbm, bf16[296,128]{1,0:T(8,128)(2,1)} %constant.20.clone.left_hbm), custom_call_target="tpu_custom_call" | custom-call | flops 1000000000 | bytes 4000000 | tf_op jit(solution)/shard_map/assemble/pallas_call | solution.py:411

commit v3 on v2

--- a/solution.py
+++ b/solution.py
@@ -26,6 +26,7 @@
 WIDE = 2 * LAGS + 128
 INPUTS = 6
 PARTS = 4
+PACKED = 12 * BANDS
 MESH = pl.DeviceIdType.MESH
 F32 = jnp.float32
 BF16 = jnp.bfloat16
@@ -108,7 +109,7 @@
     held, refs = refs[:INPUTS], refs[INPUTS:]
     x_ref, piece_ref, phase_ref, table, send_ref, flip_ref = held
     (
-    pieces, b_land, a_land, a_spec, b_spec, lre0, lim0, lre1, lim1, acc, prod, s_main, own,
+    pieces, p_land, b_land, a_land, a_spec, b_spec, lre0, lim0, lre1, lim1, acc, prod, s_main, own,
     in_sem, b_send, b_recv, a_send, a_recv, ring_send, ring_recv, sib_send, sib_recv, o_send, o_recv, m_sem, own_sem,
     ) = refs
     sta, freq = lax.axis_index("sta"), lax.axis_index("freq")
@@ -127,7 +128,8 @@
         )
 
     plane = [(dx, dh, dl) for dl in range(2) for dh in range(2) for dx in range(4)]
-    others = plane[1:]
+    plane.sort(key=lambda d: -(min(d[0], 4 - d[0]) + 2 * d[1] + d[2]))
+    others = plane[:-1]
     group = [d for d in others if d[2] == 0]
     below = ((sta + 28) % 32, freq)
     nearby = [(*d, 0) for d in others] + [(*d, 1) for d in plane]
@@ -157,24 +159,24 @@
     for n, d in enumerate(nearby):
         device = peer(*d)
         b_copies.append(
-            remote(pieces.at[device[1]], b_land.at[d[3], core, ylo, freq], b_send.at[n], b_recv.at[n], device)
+            remote(pieces.at[device[1]], p_land.at[d[3], ylo, freq], b_send.at[n], b_recv.at[n], device)
         )
     a_copies = []
     for n, d in enumerate(group):
         a_copies.append(remote(x_ref, a_land.at[freq], a_send.at[n], a_recv.at[n], peer(*d)))
     for copy in b_copies + a_copies:
         copy.start()
-    b_land[0, core, ylo, freq] = pieces[freq]
+    p_land[0, ylo, freq] = pieces[freq]
     a_land[freq] = x_ref[...]
 
     def ring(s, part):
-        y, h = part // 2, pl.ds(part % 2 * 4, 4)
+        y, h = part // 2, pl.ds(part % 2 * 48, 48)
         return remote(
             b_land.at[s, core, y, h], b_land.at[s + 1, core, y, h], ring_send.at[s, part], ring_recv.at[s, part], below
         )
 
     def across(s, part):
-        y, h = part // 2, pl.ds(part % 2 * 4, 4)
+        y, h = part // 2, pl.ds(part % 2 * 48, 48)
         return remote(
             b_land.at[s, core, y, h], b_land.at[s, core, y, h], sib_send.at[s, part], sib_recv.at[s, part], sibling
         )
@@ -189,8 +191,13 @@
 
     for copy in b_copies:
         copy.wait_recv()
-    forward(1)
-    forward(0)
+    row = lax.broadcasted_iota(jnp.int32, (PACKED, BANDS * 16), 0)
+    column = lax.broadcasted_iota(jnp.int32, (PACKED, BANDS * 16), 1)
+    pack = jnp.where(column == row % BANDS * 16 + row // BANDS, 1.0, 0.0).astype(BF16)
+    for s in (1, 0):
+        for y in range(2):
+            b_land[s, core, y] = dot(pack, p_land[s, y].reshape(BANDS * 16, 256)).astype(BF16)
+        forward(s)
 
     for copy in a_copies:
         copy.wait_recv()
@@ -208,49 +215,49 @@
     for fetch in fetches[3:]:
         fetch.wait()
 
-    def project(buffers, h, rows):
-        lre, lim = buffers
-        acc[:rows, :HALF] += dot(lre[:rows], table[h, :BAND, :HALF])
-        acc[:rows, HALF:] += dot(lim[:rows], table[h, :BAND, HALF:])
-
     def products(cross, rows):
-        acc[:rows] = jnp.zeros((rows, LAGS), F32)
-        even, odd = (lre0, lim0), (lre1, lim1)
-        cross(0, even)
-
-        def step(i, carry):
-            cross(2 * i + 1, odd)
-            project(even, 2 * i, rows)
-            cross(2 * i + 2, even)
-            project(odd, 2 * i + 1, rows)
-            return carry
-
-        lax.fori_loop(0, 3, step, 0)
-        cross(7, odd)
-        project(even, 6, rows)
-        project(odd, 7, rows)
+        buffers = ((lre0, lim0), (lre1, lim1))
+
+        def fill(two):
+            for e in range(2):
+                cross(2 * two + e, buffers[two % 2], e * BAND)
+
+        def project(two):
+            for n, part in enumerate(buffers[two % 2]):
+                columns = slice(n * HALF, n * HALF + HALF)
+                basis = table[2 * two : 2 * two + 2, :BAND, columns].reshape(2 * BAND, HALF)
+                term = dot(part[:rows], basis)
+                acc[:rows, columns] = term if two == 0 else acc[:rows, columns] + term
+
+        fill(0)
+        for two in range(BANDS // 2):
+            if two + 1 < BANDS // 2:
+                fill(two + 1)
+            project(two)
         cos, sin = acc[:rows, :HALF], acc[:rows, HALF:]
         return (cos + sin).astype(BF16), (cos - sin).astype(BF16)
 
-    def cross_unit(h, buffers):
+    def cross_unit(h, buffers, start):
         for half in range(2):
             lanes = slice(half * 256, half * 256 + 256)
+            place = slice(start + half * 256, start + half * 256 + 256)
             ar, ai = a_spec[h, 0, :, lanes], a_spec[h, 1, :, lanes]
             for two in range(PAIRS // 2):
                 re, im = [], []
                 for g in (2 * two, 2 * two + 1):
                     kk, jj = g // OWN, g % OWN
                     row = jj * 4 + half
-                    br = b_spec[h, kk, row : row + 1, :]
-                    bi = b_spec[h, kk, row + 2 : row + 3, :]
+                    br = b_spec[kk, row, h : h + 1, :]
+                    bi = b_spec[kk, row + 2, h : h + 1, :]
                     re.append(ar * br + ai * bi)
                     im.append(ai * br - ar * bi)
-                buffers[0][two * 48 : two * 48 + 48, lanes] = jnp.concatenate(re, axis=0).astype(BF16)
-                buffers[1][two * 48 : two * 48 + 48, lanes] = jnp.concatenate(im, axis=0).astype(BF16)
-
-    def cross_own(h, buffers):
+                buffers[0][two * 48 : two * 48 + 48, place] = jnp.concatenate(re, axis=0).astype(BF16)
+                buffers[1][two * 48 : two * 48 + 48, place] = jnp.concatenate(im, axis=0).astype(BF16)
+
+    def cross_own(h, buffers, start):
         for half in range(2):
             lanes = slice(half * 256, half * 256 + 256)
+            place = slice(start + half * 256, start + half * 256 + 256)
             br = a_land[h, 0, :, lanes].astype(F32)
             bi = a_land[h, 1, :, lanes].astype(F32)
             re, im = [], []
@@ -259,8 +266,8 @@
                 ai = a_spec[h, 1, pl.ds(OWN * freq + il, 1), lanes]
                 re.append(ar * br + ai * bi)
                 im.append(ai * br - ar * bi)
-            buffers[0][:96, lanes] = jnp.concatenate(re, axis=0).astype(BF16)
-            buffers[1][:96, lanes] = jnp.concatenate(im, axis=0).astype(BF16)
+            buffers[0][:96, place] = jnp.concatenate(re, axis=0).astype(BF16)
+            buffers[1][:96, place] = jnp.concatenate(im, axis=0).astype(BF16)
 
     def out_copies(unit):
         copies = []
@@ -285,7 +292,7 @@
         for kk in range(PER_UNIT):
             slot = quad + unit * PER_UNIT + 1 + kk
             spot = slot % 4
-            b_spec[:, kk] = b_land[slot // 4, spot % 2, spot // 2].astype(F32)
+            b_spec[kk] = b_land[slot // 4, spot % 2, spot // 2].astype(F32).reshape(12, BANDS, 256)
         low, high = products(cross_unit, ROWS)
         prod[:, :HALF] = dot(low, flip_ref[:HALF]).astype(BF16)
         prod[:, HALF:] = high
@@ -329,19 +336,19 @@
             across(s, part).wait_send()
 
 
-def assemble(m_hbm, own_hbm, mask_hbm, main_hbm, left_hbm, out_hbm, m, mask, main_ref, left_ref, done, in_sem, out_sem):
+def assemble(m_hbm, own_hbm, mask_hbm, main_hbm, left_hbm, out_hbm, m, mask, main_ref, left_ref, own, done, in_sem, out_sem):
     sta = lax.axis_index("sta")
-    sources = [main_hbm, left_hbm, mask_hbm] + [m_hbm.at[unit] for unit in range(UNITS)]
-    targets = [main_ref, left_ref, mask] + [m.at[unit] for unit in range(UNITS)]
+    sources = [main_hbm, left_hbm, mask_hbm, own_hbm] + [m_hbm.at[unit] for unit in range(UNITS)]
+    targets = [main_ref, left_ref, mask, own] + [m.at[unit] for unit in range(UNITS)]
     fetches = [pltpu.make_async_copy(a, b, in_sem.at[n]) for n, (a, b) in enumerate(zip(sources, targets))]
     for fetch in fetches:
         fetch.start()
-    stores = [pltpu.make_async_copy(own_hbm, out_hbm.at[0], out_sem.at[UNITS])]
+    for fetch in fetches[:4]:
+        fetch.wait()
+    stores = [pltpu.make_async_copy(own, out_hbm.at[0], out_sem.at[UNITS])]
     stores[0].start()
-    for fetch in fetches[:3]:
-        fetch.wait()
     for unit in range(UNITS):
-        fetches[3 + unit].wait()
+        fetches[4 + unit].wait()
         halves = [m[unit, :, :, half * LAGS : half * LAGS + LAGS].reshape(BANDS * 16, LAGS) for half in range(2)]
         rows = dot(main_ref[:ROWS], jnp.concatenate(halves, axis=0))
         left = dot(left_ref[: 4 * 72], m[unit, :, :, 2 * LAGS :].reshape(BANDS * 16, 128))
@@ -375,14 +382,15 @@
         scratch_shapes=[
             *[pltpu.VMEM(value.shape, value.dtype) for value in arrays],
             pltpu.VMEM((BANDS, 16, 256), BF16),
-            pltpu.VMEM((UNITS + 1, 2, 2, BANDS, 16, 256), BF16),
+            pltpu.VMEM((2, 2, BANDS, 16, 256), BF16),
+            pltpu.VMEM((UNITS + 1, 2, 2, PACKED, 256), BF16),
             pltpu.VMEM((BANDS, 2, STA, BAND), BF16),
             pltpu.VMEM((BANDS, 2, STA, BAND), F32),
-            pltpu.VMEM((BANDS, PER_UNIT, 16, 256), F32),
-            pltpu.VMEM((ROWS, BAND), BF16),
-            pltpu.VMEM((ROWS, BAND), BF16),
-            pltpu.VMEM((ROWS, BAND), BF16),
-            pltpu.VMEM((ROWS, BAND), BF16),
+            pltpu.VMEM((PER_UNIT, 12, BANDS, 256), F32),
+            pltpu.VMEM((ROWS, 2 * BAND), BF16),
+            pltpu.VMEM((ROWS, 2 * BAND), BF16),
+            pltpu.VMEM((ROWS, 2 * BAND), BF16),
+            pltpu.VMEM((ROWS, 2 * BAND), BF16),
             pltpu.VMEM((ROWS, LAGS), F32),
             pltpu.VMEM((ROWS, LAGS), BF16),
             pltpu.VMEM((UNITS, BANDS, 16, WIDE), BF16),
@@ -417,8 +425,9 @@
             pltpu.VMEM((UNITS, BANDS, 16, WIDE), BF16),
             pltpu.SMEM(pair_mask.shape, jnp.int32),
             *[pltpu.VMEM(value.shape, value.dtype) for value in selects],
+            pltpu.VMEM((OWN, STA, LAGS), BF16),
             pltpu.VMEM((UNITS, PER_UNIT, OWN, STA, LAGS), BF16),
-            dma((3 + UNITS,)),
+            dma((4 + UNITS,)),
             dma((UNITS + 1,)),
         ],
         compiler_params=pltpu.CompilerParams(vmem_limit_bytes=60 * 1024 * 1024),

time: 45 us -> 42.9 us (0.953); the launches traced: 44.7 us -> 42.2 us
  Pallas kernels: 44.7 us -> 42.2 us
    pallas_call x1, Pallas kernels: 41.3 us -> 39.1 us  [local(): pl.pallas_call(kernel, out_shape=[jax.ShapeDtypeStruct((UNITS, BANDS, 16,...]
where the time goes in v3:
time: 42.9 us; the launch traced here: 42.2 us
  Pallas kernels  42.2 us (98%)
    pallas_call x1, Pallas kernels, local(): pl.pallas_call(kernel, out_shape=[jax.ShapeDtypeStruct((UNITS, BANDS, 16,...  39.1 us
    pallas_call x1, Pallas kernels, local(): pl.pallas_call(assemble, out_shape=jax.ShapeDtypeStruct((17, OWN, STA, LA...  3.06 us

profile of v3, /device:TPU:32, one launch (start us, length us, event | category | flops | bytes accessed | tf_op | source)
XLA Modules:
  0.0 42.2 jit_solution(283381266857345110)
XLA Ops:
  0.0 39.1 %correlate.1 = (bf16[4,8,16,1152]{3,2,1,0:T(8,128)(2,1)}, bf16[3,24,512]{2,1,0:T(8,128)(2,1)}) custom-call(bf16[2,24,512]{2,1,0:T(8,128)(2,1)} %refs_0_.1, bf16[4,136,24]{2,1,0:T(8,128)(2,1)} %constant.14.clone.refs_1_, f32[16,1,512]{2,1,0:T(1,128)} %constant.15.clone.refs_2_, bf16[8,520,512]{2,1,0:T(8,128)(2,1)} %constant.16.clone.refs_3_, ...), custom_call_target="tpu_custom_call" | custom-call | flops 10000000000 | bytes 8000000 | tf_op jit(solution)/shard_map/correlate/pallas_call | solution.py:374
  39.1 3.1 %assemble.1 = bf16[17,3,24,512]{3,2,1,0:T(8,128)(2,1)} custom-call(bf16[4,8,16,1152]{3,2,1,0:T(8,128)(2,1)} %get-tuple-element.7.m_hbm, bf16[3,24,512]{2,1,0:T(8,128)(2,1)} %get-tuple-element.8.own_hbm, s32[32,32]{1,0:T(8,128)} %mask_hbm.1, bf16[296,256]{1,0:T(8,128)(2,1)} %constant.19.clone.main_hbm, bf16[296,128]{1,0:T(8,128)(2,1)} %constant.20.clone.left_hbm), custom_call_target="tpu_custom_call" | custom-call | flops 1000000000 | bytes 4000000 | tf_op jit(solution)/shard_map/assemble/pallas_call | solution.py:419

commit v4 on v3

--- a/solution.py
+++ b/solution.py
@@ -118,7 +118,7 @@
     xx, yhi = freq // 2, freq % 2
 
     fetches = [pltpu.make_async_copy(inputs[n], held[n], in_sem.at[n]) for n in range(INPUTS)]
-    for fetch in fetches:
+    for fetch in fetches[:2]:
         fetch.start()
 
     def peer(dx, dh, dl, dz=0):
@@ -132,13 +132,15 @@
     others = plane[:-1]
     group = [d for d in others if d[2] == 0]
     below = ((sta + 28) % 32, freq)
-    nearby = [(*d, 0) for d in others] + [(*d, 1) for d in plane]
+    nearby = [(*d, 1) for d in plane] + [(*d, 0) for d in others]
     sibling = (z * 4 + ylo * 2 + (1 - core), freq)
 
     barrier = pltpu.get_barrier_semaphore()
     for device in [peer(dx, dh, dl, -dz) for dx, dh, dl, dz in nearby] + [sibling]:
         pl.semaphore_signal(barrier, inc=1, device_id=device, device_id_type=MESH)
 
+    for fetch in fetches[2:]:
+        fetch.start()
     fetches[0].wait()
     fetches[1].wait()
     total = None
@@ -189,12 +191,13 @@
                 ring(s, part).start()
             across(s, part).start()
 
-    for copy in b_copies:
-        copy.wait_recv()
     row = lax.broadcasted_iota(jnp.int32, (PACKED, BANDS * 16), 0)
     column = lax.broadcasted_iota(jnp.int32, (PACKED, BANDS * 16), 1)
     pack = jnp.where(column == row % BANDS * 16 + row // BANDS, 1.0, 0.0).astype(BF16)
     for s in (1, 0):
+        for d, copy in zip(nearby, b_copies):
+            if d[3] == s:
+                copy.wait_recv()
         for y in range(2):
             b_land[s, core, y] = dot(pack, p_land[s, y].reshape(BANDS * 16, 256)).astype(BF16)
         forward(s)

time: 42.9 us -> 41.9 us (0.977); the launches traced: 42.2 us -> 41.8 us
  no operation moved by 1% of the time
where the time goes in v4:
time: 41.9 us; the launch traced here: 41.8 us
  Pallas kernels  41.8 us (100%)
    pallas_call x1, Pallas kernels, local(): pl.pallas_call(kernel, out_shape=[jax.ShapeDtypeStruct((UNITS, BANDS, 16,...  38.8 us
    pallas_call x1, Pallas kernels, local(): pl.pallas_call(assemble, out_shape=jax.ShapeDtypeStruct((17, OWN, STA, LA...  3.07 us

profile of v4, /device:TPU:32, one launch (start us, length us, event | category | flops | bytes accessed | tf_op | source)
XLA Modules:
  0.0 41.8 jit_solution(5301865390620000354)
XLA Ops:
  0.0 38.8 %correlate.1 = (bf16[4,8,16,1152]{3,2,1,0:T(8,128)(2,1)}, bf16[3,24,512]{2,1,0:T(8,128)(2,1)}) custom-call(bf16[2,24,512]{2,1,0:T(8,128)(2,1)} %refs_0_.1, bf16[4,136,24]{2,1,0:T(8,128)(2,1)} %constant.14.clone.refs_1_, f32[16,1,512]{2,1,0:T(1,128)} %constant.15.clone.refs_2_, bf16[8,520,512]{2,1,0:T(8,128)(2,1)} %constant.16.clone.refs_3_, ...), custom_call_target="tpu_custom_call" | custom-call | flops 10000000000 | bytes 8000000 | tf_op jit(solution)/shard_map/correlate/pallas_call | solution.py:377
  38.8 3.1 %assemble.1 = bf16[17,3,24,512]{3,2,1,0:T(8,128)(2,1)} custom-call(bf16[4,8,16,1152]{3,2,1,0:T(8,128)(2,1)} %get-tuple-element.7.m_hbm, bf16[3,24,512]{2,1,0:T(8,128)(2,1)} %get-tuple-element.8.own_hbm, s32[32,32]{1,0:T(8,128)} %mask_hbm.1, bf16[296,256]{1,0:T(8,128)(2,1)} %constant.19.clone.main_hbm, bf16[296,128]{1,0:T(8,128)(2,1)} %constant.20.clone.left_hbm), custom_call_target="tpu_custom_call" | custom-call | flops 1000000000 | bytes 4000000 | tf_op jit(solution)/shard_map/assemble/pallas_call | solution.py:422

commit v5 on v4

--- a/solution.py
+++ b/solution.py
@@ -350,21 +350,24 @@
         fetch.wait()
     stores = [pltpu.make_async_copy(own, out_hbm.at[0], out_sem.at[UNITS])]
     stores[0].start()
-    for unit in range(UNITS):
-        fetches[4 + unit].wait()
-        halves = [m[unit, :, :, half * LAGS : half * LAGS + LAGS].reshape(BANDS * 16, LAGS) for half in range(2)]
-        rows = dot(main_ref[:ROWS], jnp.concatenate(halves, axis=0))
-        left = dot(left_ref[: 4 * 72], m[unit, :, :, 2 * LAGS :].reshape(BANDS * 16, 128))
-        left = jnp.concatenate([left[t * 72 : t * 72 + 72] for t in range(4)], axis=1)
-        for kk in range(PER_UNIT):
-            value = rows[kk * 72 : kk * 72 + 72]
-            if kk == PER_UNIT - 1:
-                value = value + left
-            on = mask[sta, (sta + unit * PER_UNIT + 1 + kk) % 32] > 0
-            done[unit, kk] = jnp.where(on, value, 0.0).reshape(OWN, STA, LAGS).astype(BF16)
-        store = pltpu.make_async_copy(done.at[unit], out_hbm.at[pl.ds(1 + unit * PER_UNIT, PER_UNIT)], out_sem.at[unit])
-        store.start()
-        stores.append(store)
+    for pair in ((0, 1), (2, 3)):
+        for unit in pair:
+            fetches[4 + unit].wait()
+        for unit in pair:
+            halves = [m[unit, :, :, half * LAGS : half * LAGS + LAGS].reshape(BANDS * 16, LAGS) for half in range(2)]
+            rows = dot(main_ref[:ROWS], jnp.concatenate(halves, axis=0))
+            left = dot(left_ref[: 4 * 72], m[unit, :, :, 2 * LAGS :].reshape(BANDS * 16, 128))
+            left = jnp.concatenate([left[t * 72 : t * 72 + 72] for t in range(4)], axis=1)
+            for kk in range(PER_UNIT):
+                value = rows[kk * 72 : kk * 72 + 72]
+                if kk == PER_UNIT - 1:
+                    value = value + left
+                on = mask[sta, (sta + unit * PER_UNIT + 1 + kk) % 32] > 0
+                done[unit, kk] = jnp.where(on, value, 0.0).reshape(OWN, STA, LAGS).astype(BF16)
+        for unit in pair:
+            store = pltpu.make_async_copy(done.at[unit], out_hbm.at[pl.ds(1 + unit * PER_UNIT, PER_UNIT)], out_sem.at[unit])
+            store.start()
+            stores.append(store)
     for store in stores:
         store.wait()
 

time: 41.9 us -> 41.7 us (level)
  no operation moved by 1% of the time
where the time goes in v5:
time: 41.7 us; the launch traced here: 41.6 us
  Pallas kernels  41.6 us (100%)
    pallas_call x1, Pallas kernels, local(): pl.pallas_call(kernel, out_shape=[jax.ShapeDtypeStruct((UNITS, BANDS, 16,...  38.8 us
    pallas_call x1, Pallas kernels, local(): pl.pallas_call(assemble, out_shape=jax.ShapeDtypeStruct((17, OWN, STA, LA...  2.86 us

profile of v5, /device:TPU:32, one launch (start us, length us, event | category | flops | bytes accessed | tf_op | source)
XLA Modules:
  0.0 41.6 jit_solution(5153275164354711106)
XLA Ops:
  0.0 38.8 %correlate.1 = (bf16[4,8,16,1152]{3,2,1,0:T(8,128)(2,1)}, bf16[3,24,512]{2,1,0:T(8,128)(2,1)}) custom-call(bf16[2,24,512]{2,1,0:T(8,128)(2,1)} %refs_0_.1, bf16[4,136,24]{2,1,0:T(8,128)(2,1)} %constant.14.clone.refs_1_, f32[16,1,512]{2,1,0:T(1,128)} %constant.15.clone.refs_2_, bf16[8,520,512]{2,1,0:T(8,128)(2,1)} %constant.16.clone.refs_3_, ...), custom_call_target="tpu_custom_call" | custom-call | flops 10000000000 | bytes 8000000 | tf_op jit(solution)/shard_map/correlate/pallas_call | solution.py:380
  38.8 2.9 %assemble.1 = bf16[17,3,24,512]{3,2,1,0:T(8,128)(2,1)} custom-call(bf16[4,8,16,1152]{3,2,1,0:T(8,128)(2,1)} %get-tuple-element.7.m_hbm, bf16[3,24,512]{2,1,0:T(8,128)(2,1)} %get-tuple-element.8.own_hbm, s32[32,32]{1,0:T(8,128)} %mask_hbm.1, bf16[296,256]{1,0:T(8,128)(2,1)} %constant.19.clone.main_hbm, bf16[296,128]{1,0:T(8,128)(2,1)} %constant.20.clone.left_hbm), custom_call_target="tpu_custom_call" | custom-call | flops 1000000000 | bytes 4000000 | tf_op jit(solution)/shard_map/assemble/pallas_call | solution.py:425
